TPU v7x, 32 devices: a whole 2x2x4 slice. The times are simulated.
32 devices in a mesh: row: 8 (over z, y), feat: 4 (over x, core).
Axes of the slice: x: 2, y: 2, z: 4, core: 2. Of those that a mesh axis runs over, the one named last changes fastest.
Arguments:
- features: bfloat16 [28672, 512], P('row', 'feat'), may hold values from -6 to 6
- blocks: bfloat16 [896, 128, 128], P('row', 'feat'), may hold values from -0.3125 to 0.3125
- block_ptr: int32 [8, 29], P('row'), may hold values from 0 to 112, as said below
- block_col: int32 [8, 112], P('row'), may hold values from -1 to 223, as said below
- held_out: int32 [8, 128], P('row'), may hold values from 0 to 3583, as said below
- weight: bfloat16 [512, 512], P(None, 'feat'), may hold values from -0.25 to 0.25
- cotangent: bfloat16 [28672, 512], P('row', 'feat'), may hold values from -6 to 6
Outputs:
- layer_out: bfloat16 [28672, 512], P('row', 'feat')
- feature_grad: bfloat16 [28672, 512], P('row', 'feat')
- weight_grad: float32 [512, 512], P(None, 'feat')
Inputs may be any that keep to these rules, and one draw needn't show every extreme that they name: `block_ptr`: each row is nondecreasing from 0; entry 28 is the shard's number of live slots, at least 98, and 112 in some shard. `block_col`: live slots of one shard name distinct blocks, at most 14 of them in any one shard; slots at or past the live count hold -1. `held_out`: the 128 numbers of a row are distinct.
All inputs are finite; a program needn't handle non-finite values.
Results may differ from a plain program's by a relative error of at most 0.0057.
Values may be sent and summed in bfloat16 or wider, within the bound.
A program may use at most 64 MiB of HBM per device.

v0:
```python
import jax
import jax.numpy as jnp
from jax import lax
from jax.sharding import PartitionSpec as P


def body(features, blocks, block_ptr, block_col, held_out, weight, cotangent):
    shards = lax.axis_size("row")
    my_feat = lax.axis_index("feat")
    rows_dev, width_dev = features.shape
    full_blocks = lax.all_gather(blocks, "feat", axis=1, tiled=True)
    slot_count, block_size, unused_size = full_blocks.shape
    block_rows = block_ptr.shape[1] - 1
    peer_cap = (slot_count + shards - 1) // shards
    buffer_len = shards * peer_cap
    cell_ids = jnp.arange(rows_dev, dtype=jnp.int32)
    held_hits = jnp.any(cell_ids[:, None] == held_out[0][None, :], axis=1)
    kept = jnp.where(held_hits[:, None], jnp.zeros_like(features), features)
    slots = jnp.arange(slot_count, dtype=jnp.int32)
    live = slots < block_ptr[0, block_rows]
    columns = block_col[0]
    source = jnp.where(live, columns // block_rows, 0)
    local = jnp.where(live, columns % block_rows, 0)
    block_row = jnp.sum(
        (slots[:, None] >= block_ptr[0, 1:block_rows][None, :]).astype(jnp.int32), axis=1
    )
    earlier = (
        (source[:, None] == source[None, :]) & live[None, :] & (slots[None, :] < slots[:, None])
    )
    rank = jnp.sum(earlier.astype(jnp.int32), axis=1)
    position = jnp.where(live, source * peer_cap + rank, buffer_len)
    wanted = (
        jnp.full((buffer_len + 1,), -1, jnp.int32)
        .at[position]
        .set(jnp.where(live, local, -1))[:buffer_len]
    )
    asked = lax.all_to_all(wanted, "row", split_axis=0, concat_axis=0, tiled=True)
    kept_blocks = kept.reshape(block_rows, block_size, width_dev)
    outgoing = kept_blocks[jnp.clip(asked, 0, block_rows - 1)]
    outgoing = jnp.where((asked >= 0)[:, None, None], outgoing, jnp.zeros_like(outgoing))
    arrived = lax.all_to_all(outgoing, "row", split_axis=0, concat_axis=0, tiled=True)
    fetched = arrived[jnp.clip(position, 0, buffer_len - 1)]
    products = jnp.einsum("kij,kjf->kif", full_blocks, fetched, preferred_element_type=jnp.float32)
    row_select = (
        (block_row[None, :] == jnp.arange(block_rows, dtype=jnp.int32)[:, None]) & live[None, :]
    ).astype(jnp.float32)
    summed = jnp.einsum("bk,kif->bif", row_select, products, precision=lax.Precision.HIGHEST)
    aggregated = summed.reshape(rows_dev, width_dev).astype(jnp.bfloat16)
    piece = lax.all_gather(aggregated, "feat", axis=1, tiled=True)
    out_acc = jnp.dot(piece, weight, preferred_element_type=jnp.float32)
    grad_part = lax.dot_general(
        piece, cotangent, (((0,), (0,)), ((), ())), preferred_element_type=jnp.float32
    )
    grad_acc = grad_part
    out_acc, grad_terms = (out_acc, grad_acc)
    layer_out = out_acc.astype(jnp.bfloat16)
    grad_total = lax.psum(grad_terms, "row")
    weight_grad = grad_total * (1.0 / jnp.sqrt(jnp.float32(rows_dev * shards)))
    cot_piece = lax.all_gather(cotangent, "feat", axis=1, tiled=True)
    weight_piece = lax.all_gather(weight, "feat", axis=1, tiled=True)
    weight_mine = lax.dynamic_slice_in_dim(weight_piece, my_feat * width_dev, width_dev, 0)
    grad_acc = lax.dot_general(
        cot_piece, weight_mine, (((1,), (1,)), ((), ())), preferred_element_type=jnp.float32
    )
    agg_grad = grad_acc.astype(jnp.bfloat16).reshape(block_rows, block_size, width_dev)
    grad_rows = agg_grad[block_row]
    contributions = jnp.einsum(
        "kji,kjf->kif", full_blocks, grad_rows, preferred_element_type=jnp.float32
    ).astype(jnp.bfloat16)
    sending = (
        jnp.zeros((buffer_len + 1, block_size, width_dev), jnp.bfloat16)
        .at[position]
        .set(contributions)[:buffer_len]
    )
    returned = lax.all_to_all(sending, "row", split_axis=0, concat_axis=0, tiled=True)
    col_select = (asked[:, None] == jnp.arange(block_rows, dtype=jnp.int32)[None, :]).astype(
        jnp.bfloat16
    )
    grad_blocks = jnp.einsum(
        "pb,pcf->bcf", col_select, returned, preferred_element_type=jnp.float32
    )
    grad_cells = grad_blocks.reshape(rows_dev, width_dev)
    feature_grad = jnp.where(held_hits[:, None], jnp.zeros_like(grad_cells), grad_cells).astype(
        jnp.bfloat16
    )
    return (layer_out, feature_grad, weight_grad)


def solution(mesh):
    in_specs = (
        P("row", "feat"),
        P("row", "feat", None),
        P("row", None),
        P("row", None),
        P("row", None),
        P(None, "feat"),
        P("row", "feat"),
    )
    out_specs = (P("row", "feat"), P("row", "feat"), P(None, "feat"))
    return jax.shard_map(body, mesh=mesh, in_specs=in_specs, out_specs=out_specs, check_vma=False)
```

profile of v0, /device:TPU:0, one launch (start us, length us, event | category | flops | bytes accessed | tf_op | source)
XLA Modules:
  0.0 448.3 jit_solution(5567286531023250641)
XLA Ops:
  7.2 0.0 all-gather.8.cloned.1.call-start
  7.2 0.7 all-gather.8.cloned.1.call-update
  7.9 0.0 all-gather.4.cloned.1.call-start
  7.9 0.7 all-gather.4.cloned.1.call-update
  8.6 1.2 slice.13
  9.9 0.6 iota_compare_fusion.5
  10.5 1.3 fusion.23
  11.9 1.3 fusion.22
  13.2 0.2 convert_reduce_fusion
  13.4 1.3 fusion.20
  14.7 0.9 scatter_custom_fusion
  15.6 0.7 all_to_all.14
  16.3 7.3 %all-to-all-start = ((s32[8,14,1]{1,2,0:T(1,128)}), s32[8,14,1]{1,2,0:T(1,128)S(1)}, u32[]{:S(2)}, u32[]{:S(2)}) async-start(s32[8,14,1]{1,2,0:T(1,128)} %bitcast.11), calls=%async_computation | async-start | bytes 8192 | tf_op jit(solution)/shard_map/all_to_all | solution.py:37
  23.6 0.7 slice_bitcast_fusion
  24.3 0.1 convert_reduce_fusion.1
  24.4 10.6 %all_gather.14 = bf16[512,512]{1,0:T(8,128)(2,1)S(1)} all-gather(bf16[512,128]{1,0:T(8,128)(2,1)} %param.12), channel_id=1, replica_groups=mesh['row'=8,'feat'=4] {'feat'}, dimensions={1}, use_global_device_ids=true | all-gather | bytes 655360 | tf_op jit(solution)/shard_map/all_gather | solution.py:60
  35.0 12.0 %all-gather.8.cloned.1.call-done = bf16[3584,512]{1,0:T(8,128)(2,1)} async-done(((bf16[3584,128]{1,0:T(8,128)(2,1)}), bf16[3584,512]{1,0:T(8,128)(2,1)}) %all-gather.8.cloned.1.call-update) | async-done | bytes 3670032 | tf_op jit(solution)/shard_map/all_gather | solution.py:59
  47.1 3.3 fusion
  50.4 0.6 copy.36
  51.0 2.9 gather_fusion.2
  54.0 26.2 %all-gather.4.cloned.1.call-done = bf16[112,128,128]{2,1,0:T(8,128)(2,1)} async-done(((bf16[112,32,128]{2,1,0:T(8,128)(2,1)}), bf16[112,128,128]{2,1,0:T(8,128)(2,1)}) %all-gather.4.cloned.1.call-update) | async-done | bytes 3670032 | tf_op jit(solution)/shard_map/all_gather | solution.py:11
  80.2 6.3 %convert_bitcast_fusion = bf16[112,128,128]{1,2,0:T(8,128)(2,1)} fusion(bf16[112,128,128]{2,1,0:T(8,128)(2,1)} %gather_fusion.2, bf16[112,128,128]{2,1,0:T(8,128)(2,1)} %all-gather.4.cloned.1.call-done), kind=kOutput, calls=%fused_computation.10 | convolution fusion | flops 471597056 | bytes 11010048 | tf_op jit(solution)/shard_map/kji,kjf->kif/dot_general | solution.py:67
  86.5 6.1 %copy.38 = bf16[112,128,128]{2,1,0:T(8,128)(2,1)} copy(bf16[112,128,128]{1,2,0:T(8,128)(2,1)} %convert_bitcast_fusion) | data formatting | bytes 7340032 | tf_op jit(solution)/shard_map/convert_element_type | solution.py:69
  92.6 2.7 broadcast_in_dim.71
  95.3 17.2 %scatter_fusion = bf16[113,128,128]{2,1,0:T(8,128)(2,1)} fusion(bf16[113,128,128]{2,1,0:T(8,128)(2,1)} %broadcast_in_dim.71, s32[112]{0:T(128)S(1)} %fusion.18, bf16[112,128,128]{2,1,0:T(8,128)(2,1)} %copy.38), kind=kCustom, calls=%fused_computation.4 | custom fusion | bytes 11010496 | tf_op jit(solution)/shard_map/scatter | solution.py:73
  112.5 4.4 slice.22
  116.9 0.0 copy-start.3
  116.9 0.0 all-to-all-done
  116.9 5.7 %all-to-all-start.2 = ((bf16[112,128,128]{2,1,0:T(8,128)(2,1)}), bf16[112,128,128]{2,1,0:T(8,128)(2,1)}, u32[]{:S(2)}, u32[]{:S(2)}) async-start(bf16[112,128,128]{2,1,0:T(8,128)(2,1)} %slice.22), calls=%async_computation.2 | async-start | bytes 7340032 | tf_op jit(solution)/shard_map/all_to_all | solution.py:75
  122.6 0.0 copy-start.1
  122.6 0.0 copy-done.3
  122.6 0.6 fusion.4
  123.2 0.5 broadcast.269
  123.7 0.7 fusion.27
  124.4 0.1 all_to_all.16
  124.4 0.1 min.18
  124.5 80.5 %all-to-all-done.2 = bf16[112,128,128]{2,1,0:T(8,128)(2,1)} async-done(((bf16[112,128,128]{2,1,0:T(8,128)(2,1)}), bf16[112,128,128]{2,1,0:T(8,128)(2,1)}, u32[]{:S(2)}, u32[]{:S(2)}) %all-to-all-start.2) | async-done | bytes 3670048 | tf_op jit(solution)/shard_map/all_to_all | solution.py:75
  205.0 4.4 fusion.1
  209.4 0.4 copy.40
  209.8 0.0 copy-done.1
  209.8 2.7 fusion.3
  212.5 2.9 gather_fusion
  215.4 4.2 broadcast_select_fusion
  219.6 4.5 %all-to-all-start.1 = ((bf16[112,128,128]{2,1,0:T(8,128)(2,1)}), bf16[112,128,128]{2,1,0:T(8,128)(2,1)}, u32[]{:S(2)}, u32[]{:S(2)}) async-start(bf16[112,128,128]{2,1,0:T(8,128)(2,1)} %broadcast_select_fusion), calls=%async_computation.1 | async-start | bytes 7340032 | tf_op jit(solution)/shard_map/all_to_all | solution.py:41
  224.1 0.2 all-gather.6.cloned.1.call-start
  224.4 81.3 %all-to-all-done.1 = bf16[112,128,128]{2,1,0:T(8,128)(2,1)} async-done(((bf16[112,128,128]{2,1,0:T(8,128)(2,1)}), bf16[112,128,128]{2,1,0:T(8,128)(2,1)}, u32[]{:S(2)}, u32[]{:S(2)}) %all-to-all-start.1) | async-done | bytes 3670048 | tf_op jit(solution)/shard_map/all_to_all | solution.py:41
  305.7 5.0 %gather_fusion.1 = bf16[112,128,128]{2,1,0:T(8,128)(2,1)} fusion(bf16[112,128,128]{2,1,0:T(8,128)(2,1)} %all-to-all-done.1, s32[1024]{0:T(1024)S(1)} %pad_clamp_fusion.1), kind=kCustom, calls=%fused_computation.1 | custom fusion | bytes 7340480 | tf_op jit(solution)/shard_map/gather | solution.py:42
  310.7 8.8 %convolution_bitcast_fusion = f32[112,128,128]{1,2,0:T(8,128)} fusion(bf16[112,128,128]{2,1,0:T(8,128)(2,1)} %gather_fusion.1, bf16[112,128,128]{2,1,0:T(8,128)(2,1)} %all-gather.4.cloned.1.call-done), kind=kOutput, calls=%fused_computation.12 | convolution fusion | flops 469762048 | bytes 14680064 | tf_op jit(solution)/shard_map/kij,kjf->kif/dot_general | solution.py:43
  319.5 8.4 %copy.34 = f32[112,128,128]{2,0,1:T(8,128)} copy(f32[112,128,128]{1,2,0:T(8,128)} %convolution_bitcast_fusion) | data formatting | bytes 14680064 | tf_op jit(solution)/shard_map/kij,kjf->kif/dot_general | solution.py:43
  327.9 0.0 copy-start
  327.9 6.0 %convolution_convert_fusion.2 = bf16[28,128,128]{2,0,1:T(8,128)(2,1)S(1)} fusion(f32[112,128,128]{2,0,1:T(8,128)} %copy.34, s32[112]{0:T(128)S(1)} %convert_reduce_fusion.1, pred[112]{0:T(512)(128)(4,1)S(1)} %iota_compare_fusion.5), kind=kOutput, calls=%fused_computation.17 | convolution fusion | flops 617027712 | bytes 8258096 | tf_op jit(solution)/shard_map/bk,kif->bif/dot_general | solution.py:47
  333.9 0.0 copy-start.2
  333.9 1.3 copy.35
  335.2 0.0 all-gather.6.cloned.1.call-update
  335.2 0.0 all-reduce.2.cloned.1.call-start
  335.3 30.2 %all-gather.6.cloned.1.call-done = bf16[3584,512]{1,0:T(8,128)(2,1)} async-done(((bf16[3584,128]{1,0:T(8,128)(2,1)}), bf16[3584,512]{1,0:T(8,128)(2,1)}) %all-gather.6.cloned.1.call-update) | async-done | bytes 3670032 | tf_op jit(solution)/shard_map/all_gather | solution.py:49
  365.5 0.0 copy-done
  365.5 3.9 fusion.28
  369.4 0.0 all-reduce.2.cloned.1.call-update
  369.4 0.0 copy-done.2
  369.4 4.1 convolution_convert_fusion.1
  373.5 66.6 %all-reduce.2.cloned.1.call-done = f32[512,128]{1,0:T(8,128)} async-done(((f32[512,128]{1,0:T(8,128)}), f32[512,128]{1,0:T(8,128)}) %all-reduce.2.cloned.1.call-update) | async-done | bytes 262160 | tf_op jit(solution)/shard_map/psum | solution.py:57
  440.1 1.7 broadcast_multiply_fusion
  (7 shorter events, 0.0 us)
Async XLA Ops:
  7.2 39.9 %all-gather.8.cloned.1.call-start = ((), (), s32[]{:S(2)}) async-start(), calls=%async_computation.5 | async-start | bytes 4587520 | tf_op jit(solution)/shard_map/all_gather | solution.py:59
  7.9 72.3 %all-gather.4.cloned.1.call-start = ((), (), s32[]{:S(2)}) async-start(), calls=%async_computation.3 | async-start | bytes 4587520 | tf_op jit(solution)/shard_map/all_gather | solution.py:11
  16.3 100.6 %all-to-all-start = ((s32[8,14,1]{1,2,0:T(1,128)}), s32[8,14,1]{1,2,0:T(1,128)S(1)}, u32[]{:S(2)}, u32[]{:S(2)}) async-start(s32[8,14,1]{1,2,0:T(1,128)} %bitcast.11), calls=%async_computation | async-start | bytes 8192 | tf_op jit(solution)/shard_map/all_to_all | solution.py:37
  116.9 5.7 %copy-start.3 = (s32[1,128]{1,0:T(1,128)S(1)}, s32[1,128]{1,0:T(1,128)}, u32[]{:S(2)}) copy-start(s32[1,128]{1,0:T(1,128)} %param.11) | copy-start | bytes 1540
  116.9 88.1 %all-to-all-start.2 = ((bf16[112,128,128]{2,1,0:T(8,128)(2,1)}), bf16[112,128,128]{2,1,0:T(8,128)(2,1)}, u32[]{:S(2)}, u32[]{:S(2)}) async-start(bf16[112,128,128]{2,1,0:T(8,128)(2,1)} %slice.22), calls=%async_computation.2 | async-start | bytes 7340032 | tf_op jit(solution)/shard_map/all_to_all | solution.py:75
  122.6 87.2 %copy-start.1 = (bf16[3584,128]{1,0:T(8,128)(2,1)S(1)}, bf16[3584,128]{1,0:T(8,128)(2,1)}, u32[]{:S(2)}) copy-start(bf16[3584,128]{1,0:T(8,128)(2,1)} %param.7) | copy-start | bytes 2752516
  219.6 86.0 %all-to-all-start.1 = ((bf16[112,128,128]{2,1,0:T(8,128)(2,1)}), bf16[112,128,128]{2,1,0:T(8,128)(2,1)}, u32[]{:S(2)}, u32[]{:S(2)}) async-start(bf16[112,128,128]{2,1,0:T(8,128)(2,1)} %broadcast_select_fusion), calls=%async_computation.1 | async-start | bytes 7340032 | tf_op jit(solution)/shard_map/all_to_all | solution.py:41
  224.1 141.3 %all-gather.6.cloned.1.call-start = ((), (), s32[]{:S(2)}) async-start(), calls=%async_computation.4 | async-start | bytes 4587520 | tf_op jit(solution)/shard_map/all_gather | solution.py:49
  327.9 37.5 %copy-start = (bf16[3584,128]{1,0:T(8,128)(2,1)S(1)}, bf16[3584,128]{1,0:T(8,128)(2,1)}, u32[]{:S(2)}) copy-start(bf16[3584,128]{1,0:T(8,128)(2,1)} %param.13) | copy-start | bytes 2752516
  333.9 35.5 %copy-start.2 = (bf16[512,128]{1,0:T(8,128)(2,1)S(1)}, bf16[512,128]{1,0:T(8,128)(2,1)}, u32[]{:S(2)}) copy-start(bf16[512,128]{1,0:T(8,128)(2,1)} %param.12) | copy-start | bytes 393220
  335.2 104.9 %all-reduce.2.cloned.1.call-start = ((), (), s32[]{:S(2)}) async-start(), calls=%async_computation.6 | async-start | bytes 524288 | tf_op jit(solution)/shard_map/psum | solution.py:57
Sparse Core Ops, SparseCore 0:
  9.5 37.4 all-gather.7
  48.6 31.4 all-gather.3
  335.3 30.0 all-gather.5
  369.5 70.5 all-reduce.1
where the time goes:
time: 449 us; the launch traced here: 448 us
  waiting for transfers between devices  298 us (66%)
  local copies, waits for them, and re-layouts  56.2 us (13%)
  matrix products  36.8 us (8%)
  starting transfers between devices  17.8 us (4%)
  other arithmetic  14.7 us (3%)
  between operations  13.9 us (3%)
  blocking collectives  10.6 us (2%)
    all_to_all x1, waiting for transfers between devices, body(): lax.all_to_all(outgoing, 'row', split_axis=0, concat_axis=0, tiled=True)  81.3 us
    all_to_all x1, waiting for transfers between devices, body(): lax.all_to_all(sending, 'row', split_axis=0, concat_axis=0, tiled=True)  80.5 us
    psum x1, waiting for transfers between devices, body(): grad_total = lax.psum(grad_terms, 'row')  66.6 us
    all_gather x1, waiting for transfers between devices, body(): piece = lax.all_gather(aggregated, 'feat', axis=1, tiled=True)  30.2 us
    all_gather x1, waiting for transfers between devices, body(): full_blocks = lax.all_gather(blocks, 'feat', axis=1, tiled=True)  26.2 us
    scatter x1, local copies, waits for them, and re-layouts, body(): sending = jnp.zeros((buffer_len + 1, block_size, width_dev), jnp.bfloat16...  17.2 us
    all_gather x1, waiting for transfers between devices, body(): cot_piece = lax.all_gather(cotangent, 'feat', axis=1, tiled=True)  12 us
    all_gather x1, blocking collectives, body(): weight_piece = lax.all_gather(weight, 'feat', axis=1, tiled=True)  10.6 us
  transfers between devices with their start and end apart: 7, of which 6 were waited for; matrix products, arithmetic and copies ran while one was open for 13% of the time, Pallas kernels for 0%

commit v1 on v0

v1 whole, which is shorter than its diff:
```python
import jax
import jax.numpy as jnp
from jax import lax
from jax.experimental import pallas as pl
from jax.experimental.pallas import tpu as pltpu
from jax.sharding import PartitionSpec as P

VMEM_LIMIT = 40 * 2**20


def local_call(kernel, scalars, operands, out_shape, scratch=(), flops=0):
    moved = sum(o.size * o.dtype.itemsize for o in operands)
    moved += out_shape.size * out_shape.dtype.itemsize
    return pl.pallas_call(
        kernel,
        out_shape=out_shape,
        grid_spec=pltpu.PrefetchScalarGridSpec(
            num_scalar_prefetch=len(scalars),
            grid=(),
            in_specs=[pl.BlockSpec(memory_space=pltpu.VMEM)] * len(operands),
            out_specs=pl.BlockSpec(memory_space=pltpu.VMEM),
            scratch_shapes=list(scratch),
        ),
        compiler_params=pltpu.CompilerParams(vmem_limit_bytes=VMEM_LIMIT),
        cost_estimate=pl.CostEstimate(flops=flops, bytes_accessed=moved, transcendentals=0),
    )(*scalars, *operands)


def held_rows(held_ref, b, block_size):
    held = held_ref[...]
    ids = b * block_size + lax.broadcasted_iota(jnp.int32, (block_size, held.shape[1]), 0)
    return jnp.max((ids == held).astype(jnp.float32), axis=1, keepdims=True) > 0.5


def pack_kernel(asked_ref, held_ref, features_ref, out_ref, kept_ref):
    block_rows, block_size, _ = features_ref.shape

    def keep(b, carry):
        rows = features_ref[b].astype(jnp.float32)
        hit = held_rows(held_ref, b, block_size)
        kept_ref[b] = jnp.where(hit, 0.0, rows).astype(kept_ref.dtype)
        return carry

    lax.fori_loop(0, block_rows, keep, 0, unroll=4)

    def copy(p, carry):
        out_ref[p] = kept_ref[jnp.maximum(asked_ref[p], 0)]
        return carry

    lax.fori_loop(0, out_ref.shape[0], copy, 0, unroll=8)


def forward_kernel(position_ref, brow_ref, blocks_ref, arrived_ref, out_ref, acc_ref):
    slot_count = blocks_ref.shape[0]
    acc_ref[...] = jnp.zeros_like(acc_ref)

    def step(g, carry):
        slots = [g * UNROLL + i for i in range(UNROLL)]
        parts = [
            jnp.dot(blocks_ref[k], arrived_ref[position_ref[k]], preferred_element_type=jnp.float32)
            for k in slots
        ]
        for k, part in zip(slots, parts):
            acc_ref[brow_ref[k]] += part
        return carry

    lax.fori_loop(0, slot_count // UNROLL, step, 0)
    for k in range(slot_count // UNROLL * UNROLL, slot_count):
        acc_ref[brow_ref[k]] += jnp.dot(
            blocks_ref[k], arrived_ref[position_ref[k]], preferred_element_type=jnp.float32
        )

    def emit(b, carry):
        out_ref[b] = acc_ref[b].astype(out_ref.dtype)
        return carry

    lax.fori_loop(0, out_ref.shape[0], emit, 0, unroll=4)


UNROLL = 8


def contribution_kernel(slot_ref, brow_ref, blocks_ref, grad_ref, out_ref):
    def one(p):
        out_ref[p] = lax.dot_general(
            blocks_ref[slot_ref[p]],
            grad_ref[brow_ref[p]],
            (((0,), (0,)), ((), ())),
            preferred_element_type=jnp.float32,
        ).astype(out_ref.dtype)

    def step(p, carry):
        one(p)
        return carry

    lax.fori_loop(0, out_ref.shape[0], step, 0, unroll=8)


def collect_kernel(asked_ref, held_ref, returned_ref, out_ref, acc_ref):
    block_rows, block_size, _ = out_ref.shape
    acc_ref[...] = jnp.zeros_like(acc_ref)

    def add(p, carry):
        to = jnp.where(asked_ref[p] < 0, block_rows, asked_ref[p])
        acc_ref[to] += returned_ref[p].astype(jnp.float32)
        return carry

    lax.fori_loop(0, returned_ref.shape[0], add, 0, unroll=8)

    def emit(b, carry):
        hit = held_rows(held_ref, b, block_size)
        out_ref[b] = jnp.where(hit, 0.0, acc_ref[b]).astype(out_ref.dtype)
        return carry

    lax.fori_loop(0, block_rows, emit, 0, unroll=4)


def body(features, blocks, block_ptr, block_col, held_out, weight, cotangent):
    shards = lax.axis_size("row")
    my_feat = lax.axis_index("feat")
    rows_dev, width_dev = features.shape
    slot_count = blocks.shape[0]
    block_size = blocks.shape[2]
    block_rows = block_ptr.shape[1] - 1
    peer_cap = (slot_count + shards - 1) // shards
    buffer_len = shards * peer_cap
    bf16, f32 = jnp.bfloat16, jnp.float32

    slots = jnp.arange(slot_count, dtype=jnp.int32)
    live = slots < block_ptr[0, block_rows]
    columns = block_col[0]
    source = jnp.where(live, columns // block_rows, 0)
    local = jnp.where(live, columns % block_rows, 0)
    block_row = jnp.sum(
        (slots[:, None] >= block_ptr[0, 1:block_rows][None, :]).astype(jnp.int32), axis=1
    )
    earlier = (
        (source[:, None] == source[None, :]) & live[None, :] & (slots[None, :] < slots[:, None])
    )
    rank = jnp.sum(earlier.astype(jnp.int32), axis=1)
    position = jnp.where(live, source * peer_cap + rank, -1)
    places = jnp.arange(buffer_len, dtype=jnp.int32)
    match = (places[:, None] == position[None, :]).astype(jnp.int32)
    wanted = jnp.sum(match * (local[None, :] + 1), axis=1) - 1
    slot_at = jnp.sum(match * slots[None, :], axis=1)
    brow_at = jnp.sum(match * block_row[None, :], axis=1)
    asked = lax.all_to_all(wanted, "row", split_axis=0, concat_axis=0, tiled=True)

    full_blocks = lax.all_gather(blocks, "feat", axis=1, tiled=True)
    block_shape = (block_size, width_dev)
    outgoing = local_call(
        pack_kernel,
        (asked,),
        (held_out, features.reshape(block_rows, *block_shape)),
        jax.ShapeDtypeStruct((buffer_len, *block_shape), bf16),
        (pltpu.VMEM((block_rows, *block_shape), bf16),),
    )
    arrived = lax.all_to_all(outgoing, "row", split_axis=0, concat_axis=0, tiled=True)

    cot_piece = lax.all_gather(cotangent, "feat", axis=1, tiled=True)
    weight_piece = lax.all_gather(weight, "feat", axis=1, tiled=True)
    weight_mine = lax.dynamic_slice_in_dim(weight_piece, my_feat * width_dev, width_dev, 0)
    agg_grad = lax.dot_general(
        cot_piece, weight_mine, (((1,), (1,)), ((), ())), preferred_element_type=f32
    ).astype(bf16)
    sending = local_call(
        contribution_kernel,
        (slot_at, brow_at),
        (full_blocks, agg_grad.reshape(block_rows, *block_shape)),
        jax.ShapeDtypeStruct((buffer_len, *block_shape), bf16),
        flops=2 * buffer_len * block_size * block_size * width_dev,
    )
    returned = lax.all_to_all(sending, "row", split_axis=0, concat_axis=0, tiled=True)

    aggregated = local_call(
        forward_kernel,
        (jnp.maximum(position, 0), jnp.where(live, block_row, block_rows)),
        (full_blocks, arrived),
        jax.ShapeDtypeStruct((block_rows, *block_shape), bf16),
        (pltpu.VMEM((block_rows + 1, *block_shape), f32),),
        flops=2 * slot_count * block_size * block_size * width_dev,
    ).reshape(rows_dev, width_dev)
    piece = lax.all_gather(aggregated, "feat", axis=1, tiled=True)
    layer_out = jnp.dot(piece, weight, preferred_element_type=f32).astype(bf16)
    grad_part = lax.dot_general(
        piece, cotangent, (((0,), (0,)), ((), ())), preferred_element_type=f32
    )
    grad_total = lax.psum(grad_part, "row")
    weight_grad = grad_total * (1.0 / jnp.sqrt(f32(rows_dev * shards)))

    feature_grad = local_call(
        collect_kernel,
        (asked,),
        (held_out, returned),
        jax.ShapeDtypeStruct((block_rows, *block_shape), bf16),
        (pltpu.VMEM((block_rows + 1, *block_shape), f32),),
    ).reshape(rows_dev, width_dev)
    return (layer_out, feature_grad, weight_grad)


def solution(mesh):
    in_specs = (
        P("row", "feat"),
        P("row", "feat", None),
        P("row", None),
        P("row", None),
        P("row", None),
        P(None, "feat"),
        P("row", "feat"),
    )
    out_specs = (P("row", "feat"), P("row", "feat"), P(None, "feat"))
    return jax.shard_map(body, mesh=mesh, in_specs=in_specs, out_specs=out_specs, check_vma=False)
```

time: 449 us -> 295 us (0.66)
  waiting for transfers between devices: 298 us -> 199 us
  local copies, waits for them, and re-layouts: 56.2 us -> 12.9 us
  matrix products: 36.8 us -> 11.3 us
  Pallas kernels: 0 us -> 18.7 us
  blocking collectives: 10.6 us -> 20.7 us
  starting transfers between devices: 17.8 us -> 9.28 us
  other arithmetic: 14.7 us -> 8.02 us
    all_to_all x1, waiting for transfers between devices: 81.3 us -> 35.3 us  [body(): lax.all_to_all(outgoing, 'row', split_axis=0, concat_axis=0, tiled=True)]
    all_gather x1, waiting for transfers between devices: 30.2 us -> 0.01 us  [body(): piece = lax.all_gather(aggregated, 'feat', axis=1, tiled=True)]
    dot_general x5 -> x1, matrix products: 29.6 us -> 4.08 us  [body(): layer_out = jnp.dot(piece, weight, preferred_element_type=f32).astype(bf16)]
    pallas_call x0 -> x4, Pallas kernels: none -> 18.7 us  [local_call(): pl.pallas_call(kernel, out_shape=out_shape, grid_spec=pltpu.PrefetchScala...]
    scatter x2 -> x0, local copies, waits for them, and re-layouts: 18.1 us -> none  [the longest x1 17.2 us: body(): sending = jnp.zeros((buffer_len + 1, block_size, width_dev), jnp.bfloat16...]
    all_to_all x0 -> x1, blocking collectives: none -> 13.5 us  [body(): lax.all_to_all(wanted, 'row', split_axis=0, concat_axis=0, tiled=True)]
    all_gather x1, waiting for transfers between devices: 12 us -> 0.01 us  [body(): cot_piece = lax.all_gather(cotangent, 'feat', axis=1, tiled=True)]
    gather x3 -> x0, local copies, waits for them, and re-layouts: 10.8 us -> none  [the longest x1 5.02 us: body(): fetched = arrived[jnp.clip(position, 0, buffer_len - 1)]]
  transfers between devices with their start and end apart: 7 -> 6, of which waited for: 6 -> 4; matrix products, arithmetic and copies ran while one was open for 13% -> 6% of each run, Pallas kernels for 0% -> 6%
where the time goes in v1:
time: 295 us; the launch traced here: 294 us
  waiting for transfers between devices  199 us (67%)
  blocking collectives  20.7 us (7%)
  Pallas kernels  18.7 us (6%)
  between operations  13.9 us (5%)
  local copies, waits for them, and re-layouts  12.9 us (4%)
  matrix products  11.3 us (4%)
  starting transfers between devices  9.28 us (3%)
  other arithmetic  8.02 us (3%)
    all_to_all x1, waiting for transfers between devices, body(): lax.all_to_all(sending, 'row', split_axis=0, concat_axis=0, tiled=True)  71.5 us
    psum x1, waiting for transfers between devices, body(): grad_total = lax.psum(grad_part, 'row')  65.7 us
    all_to_all x1, waiting for transfers between devices, body(): lax.all_to_all(outgoing, 'row', split_axis=0, concat_axis=0, tiled=True)  35.3 us
    all_gather x1, waiting for transfers between devices, body(): full_blocks = lax.all_gather(blocks, 'feat', axis=1, tiled=True)  25.3 us
    pallas_call x4, Pallas kernels, local_call(): pl.pallas_call(kernel, out_shape=out_shape, grid_spec=pltpu.PrefetchScala...  18.7 us
    all_to_all x1, blocking collectives, body(): lax.all_to_all(wanted, 'row', split_axis=0, concat_axis=0, tiled=True)  13.5 us
    unnamed x18, local copies, waits for them, and re-layouts  9.64 us
    all_gather x1, blocking collectives, body(): weight_piece = lax.all_gather(weight, 'feat', axis=1, tiled=True)  7.2 us
  transfers between devices with their start and end apart: 6, of which 4 were waited for; matrix products, arithmetic and copies ran while one was open for 6% of the time, Pallas kernels for 6%

profile of v1, /device:TPU:0, one launch (start us, length us, event | category | flops | bytes accessed | tf_op | source)
XLA Modules:
  0.0 294.1 jit_solution(17575126569986825348)
XLA Ops:
  7.2 0.0 all-gather.8.cloned.1.call-start
  7.2 0.7 all-gather.8.cloned.1.call-update
  7.9 1.2 slice.6
  9.1 0.6 iota_compare_fusion.4
  9.8 0.7 slice_bitcast_fusion
  10.5 0.1 convert_reduce_fusion.1
  10.6 1.3 fusion.5
  11.9 1.3 fusion.9
  13.2 0.2 convert_reduce_fusion
  13.4 1.3 add_bitcast_fusion
  14.8 0.1 select_reduce_fusion
  14.9 0.1 sub.17
  15.0 13.5 %all_to_all.18 = s32[8,14,1]{1,2,0:T(1,128)S(1)} all-to-all(s32[8,14,1]{1,2,0:T(1,128)S(1)} %bitcast.37), channel_id=1, replica_groups=mesh['row'=8,'feat'=4] {'row'}, dimensions={0} | all-to-all | bytes 896 | tf_op jit(solution)/shard_map/all_to_all | solution.py:147
  28.5 0.5 broadcast.108
  29.0 0.7 reduce.3
  29.7 0.1 all_to_all.12.asked_ref
  29.8 0.0 copy-start.4
  29.8 1.2 copy-done.4
  31.0 0.0 copy-start.5
  31.0 0.7 copy-done.5
  31.6 1.9 shard_map.94
  33.5 0.0 copy-start
  33.5 1.9 copy-done
  35.4 0.0 copy-start.8
  35.4 4.6 %all-to-all-start.1 = ((bf16[112,128,128]{2,1,0:T(8,128)(2,1)}), bf16[112,128,128]{2,1,0:T(8,128)(2,1)}, u32[]{:S(2)}, u32[]{:S(2)}) async-start(bf16[112,128,128]{2,1,0:T(8,128)(2,1)} %copy-done), calls=%async_computation.1 | async-start | bytes 7340032 | tf_op jit(solution)/shard_map/all_to_all | solution.py:158
  40.1 0.0 all-gather.4.cloned.1.call-start
  40.1 0.7 all-gather.4.cloned.1.call-update
  40.8 0.0 copy-done.8
  40.9 7.2 %all_gather.14 = bf16[512,512]{1,0:T(8,128)(2,1)S(1)} all-gather(bf16[512,128]{1,0:T(8,128)(2,1)S(1)} %copy-done.8), channel_id=1, replica_groups=mesh['row'=8,'feat'=4] {'feat'}, dimensions={1}, use_global_device_ids=true | all-gather | bytes 655360 | tf_op jit(solution)/shard_map/all_gather | solution.py:161
  48.1 0.0 all-gather.8.cloned.1.call-done
  48.1 3.4 %fusion = bf16[3584,128]{0,1:T(8,128)(2,1)S(1)} fusion(bf16[3584,512]{1,0:T(8,128)(2,1)} %all-gather.8.cloned.1.call-done, bf16[512,512]{1,0:T(8,128)(2,1)S(1)} %all_gather.14, s32[]{:T(128)S(6)} %select_n.58), kind=kOutput, calls=%fused_computation.2 | convolution fusion | flops 470220800 | bytes 4718596 | tf_op jit(solution)/shard_map/dot_general | solution.py:163
  51.4 0.6 copy.14
  52.0 25.3 %all-gather.4.cloned.1.call-done.blocks_ref = bf16[112,128,128]{2,1,0:T(8,128)(2,1)} async-done(((bf16[112,32,128]{2,1,0:T(8,128)(2,1)}), bf16[112,128,128]{2,1,0:T(8,128)(2,1)}) %all-gather.4.cloned.1.call-update) | async-done | bytes 3670032 | tf_op jit(solution)/shard_map/all_gather | solution.py:149
  77.4 0.0 copy-start.2
  77.4 2.0 copy-done.2
  79.4 4.3 %shard_map.96 = bf16[112,128,128]{2,1,0:T(8,128)(2,1)S(1)} custom-call(s32[112]{0:T(128)S(1)} %get-tuple-element.4.slot_ref, s32[112]{0:T(128)S(1)} %get-tuple-element.3.brow_ref, bf16[112,128,128]{2,1,0:T(8,128)(2,1)S(1)} %copy-done.2, bf16[28,128,128]{2,1,0:T(8,128)(2,1)S(1)} %bitcast.34), custom_call_target="tpu_custom_call" | custom-call | flops 469762048 | bytes 8257536 | tf_op jit(solution)/shard_map/pallas_call | solution.py:14
  83.7 0.0 copy-start.1
  83.7 1.8 copy-done.1
  85.5 35.3 %all-to-all-done.1.arrived_ref = bf16[112,128,128]{2,1,0:T(8,128)(2,1)} async-done(((bf16[112,128,128]{2,1,0:T(8,128)(2,1)}), bf16[112,128,128]{2,1,0:T(8,128)(2,1)}, u32[]{:S(2)}, u32[]{:S(2)}) %all-to-all-start.1) | async-done | bytes 3670048 | tf_op jit(solution)/shard_map/all_to_all | solution.py:158
  120.9 4.5 %all-to-all-start.2 = ((bf16[112,128,128]{2,1,0:T(8,128)(2,1)}), bf16[112,128,128]{2,1,0:T(8,128)(2,1)}, u32[]{:S(2)}, u32[]{:S(2)}) async-start(bf16[112,128,128]{2,1,0:T(8,128)(2,1)} %copy-done.1), calls=%async_computation.2 | async-start | bytes 7340032 | tf_op jit(solution)/shard_map/all_to_all | solution.py:173
  125.4 0.0 all-gather.6.cloned.1.call-start
  125.4 0.7 select_maximum_fusion
  126.1 0.0 copy-start.3
  126.1 2.0 copy-done.3
  128.1 0.0 copy-start.6
  128.1 7.0 %shard_map.95 = bf16[28,128,128]{2,1,0:T(8,128)(2,1)} custom-call(s32[112]{0:T(128)S(1)} %get-tuple-element.10.position_ref, s32[112]{0:T(128)S(1)} %get-tuple-element.11.brow_ref, bf16[112,128,128]{2,1,0:T(8,128)(2,1)S(1)} %copy-done.3, bf16[112,128,128]{2,1,0:T(8,128)(2,1)} %all-to-all-done.1.arrived_ref), custom_call_target="tpu_custom_call" | custom-call | flops 469762048 | bytes 8257536 | tf_op jit(solution)/shard_map/pallas_call | solution.py:14
  135.2 0.0 copy-start.7
  135.2 0.0 all-gather.6.cloned.1.call-update
  135.2 0.0 all-reduce.2.cloned.1.call-start
  135.2 71.5 %all-to-all-done.2.returned_ref = bf16[112,128,128]{2,1,0:T(8,128)(2,1)} async-done(((bf16[112,128,128]{2,1,0:T(8,128)(2,1)}), bf16[112,128,128]{2,1,0:T(8,128)(2,1)}, u32[]{:S(2)}, u32[]{:S(2)}) %all-to-all-start.2) | async-done | bytes 3670048 | tf_op jit(solution)/shard_map/all_to_all | solution.py:173
  206.7 0.0 copy-done.6
  206.7 5.5 %shard_map.97 = bf16[28,128,128]{2,1,0:T(8,128)(2,1)} custom-call(s32[112]{0:T(128)S(1)} %all_to_all.12.asked_ref, s32[1,128]{1,0:T(1,128)S(1)} %copy-done.6, bf16[112,128,128]{2,1,0:T(8,128)(2,1)} %all-to-all-done.2.returned_ref), custom_call_target="tpu_custom_call" | custom-call | bytes 4588032 | tf_op jit(solution)/shard_map/pallas_call | solution.py:14
  212.2 0.0 all-gather.6.cloned.1.call-done
  212.2 0.0 copy-done.7
  212.2 3.9 %fusion.10 = f32[512,128]{1,0:T(8,128)} fusion(bf16[3584,512]{1,0:T(8,128)(2,1)} %all-gather.6.cloned.1.call-done, bf16[3584,128]{1,0:T(8,128)(2,1)S(1)} %copy-done.7), kind=kOutput, calls=%fused_computation.34 | convolution fusion | flops 469762048 | bytes 4849664 | tf_op jit(solution)/shard_map/dot_general | solution.py:185
  216.1 0.0 all-reduce.2.cloned.1.call-update
  216.2 4.1 %convolution_convert_fusion.1 = bf16[3584,128]{1,0:T(8,128)(2,1)} fusion(bf16[3584,512]{1,0:T(8,128)(2,1)} %all-gather.6.cloned.1.call-done, bf16[512,128]{1,0:T(8,128)(2,1)S(1)} %copy-done.8), kind=kOutput, calls=%fused_computation.1 | convolution fusion | flops 470220800 | bytes 4718592 | tf_op jit(solution)/shard_map/dot_general | solution.py:184
  220.2 65.7 %all-reduce.2.cloned.1.call-done = f32[512,128]{1,0:T(8,128)} async-done(((f32[512,128]{1,0:T(8,128)}), f32[512,128]{1,0:T(8,128)}) %all-reduce.2.cloned.1.call-update) | async-done | bytes 262160 | tf_op jit(solution)/shard_map/psum | solution.py:188
  285.9 1.7 broadcast_multiply_fusion
  (1 shorter events, 0.0 us)
Async XLA Ops:
  7.2 40.9 %all-gather.8.cloned.1.call-start = ((), (), s32[]{:S(2)}) async-start(), calls=%async_computation.5 | async-start | bytes 4587520 | tf_op jit(solution)/shard_map/all_gather | solution.py:160
  29.8 1.2 copy-start.4
  31.0 0.7 copy-start.5
  33.5 1.9 copy-start
  35.4 5.4 %copy-start.8 = (bf16[512,128]{1,0:T(8,128)(2,1)S(1)}, bf16[512,128]{1,0:T(8,128)(2,1)}, u32[]{:S(2)}) copy-start(bf16[512,128]{1,0:T(8,128)(2,1)} %param.12) | copy-start | bytes 393220
  35.4 85.4 %all-to-all-start.1 = ((bf16[112,128,128]{2,1,0:T(8,128)(2,1)}), bf16[112,128,128]{2,1,0:T(8,128)(2,1)}, u32[]{:S(2)}, u32[]{:S(2)}) async-start(bf16[112,128,128]{2,1,0:T(8,128)(2,1)} %copy-done), calls=%async_computation.1 | async-start | bytes 7340032 | tf_op jit(solution)/shard_map/all_to_all | solution.py:158
  40.1 37.3 %all-gather.4.cloned.1.call-start = ((), (), s32[]{:S(2)}) async-start(), calls=%async_computation.3 | async-start | bytes 4587520 | tf_op jit(solution)/shard_map/all_gather | solution.py:149
  77.4 2.0 copy-start.2
  83.7 1.8 copy-start.1
  120.9 85.9 %all-to-all-start.2 = ((bf16[112,128,128]{2,1,0:T(8,128)(2,1)}), bf16[112,128,128]{2,1,0:T(8,128)(2,1)}, u32[]{:S(2)}, u32[]{:S(2)}) async-start(bf16[112,128,128]{2,1,0:T(8,128)(2,1)} %copy-done.1), calls=%async_computation.2 | async-start | bytes 7340032 | tf_op jit(solution)/shard_map/all_to_all | solution.py:173
  125.4 86.9 %all-gather.6.cloned.1.call-start = ((), (), s32[]{:S(2)}) async-start(), calls=%async_computation.4 | async-start | bytes 4587520 | tf_op jit(solution)/shard_map/all_gather | solution.py:183
  126.1 2.0 copy-start.3
  128.1 78.6 %copy-start.6 = (s32[1,128]{1,0:T(1,128)S(1)}, s32[1,128]{1,0:T(1,128)}, u32[]{:S(2)}) copy-start(s32[1,128]{1,0:T(1,128)} %held_ref.3) | copy-start | bytes 1540
  135.2 77.1 %copy-start.7 = (bf16[3584,128]{1,0:T(8,128)(2,1)S(1)}, bf16[3584,128]{1,0:T(8,128)(2,1)}, u32[]{:S(2)}) copy-start(bf16[3584,128]{1,0:T(8,128)(2,1)} %param.13) | copy-start | bytes 2752516
  135.2 150.7 %all-reduce.2.cloned.1.call-start = ((), (), s32[]{:S(2)}) async-start(), calls=%async_computation.6 | async-start | bytes 524288 | tf_op jit(solution)/shard_map/psum | solution.py:188
Sparse Core Ops, SparseCore 0:
  9.5 34.8 all-gather.7
  46.0 31.3 all-gather.3
  135.3 33.2 all-gather.5
  216.3 69.5 all-reduce.1

commit v2 on v1

--- a/solution.py
+++ b/solution.py
@@ -115,6 +115,76 @@
     lax.fori_loop(0, block_rows, emit, 0, unroll=4)
 
 
+def sum_kernel(shards, part_ref, out_ref, terms_ref, total_ref, sent1, got1, sent2, got2):
+    rows = part_ref.shape[0] // shards
+    me = lax.axis_index("row")
+    peers = [lax.rem(me + d, shards) for d in range(1, shards)]
+    barrier = pltpu.get_barrier_semaphore()
+    for peer in peers:
+        pl.semaphore_signal(
+            barrier, inc=1, device_id={"row": peer}, device_id_type=pl.DeviceIdType.MESH
+        )
+    pl.semaphore_wait(barrier, shards - 1)
+
+    def span(owner):
+        return pl.ds(pl.multiple_of(owner * rows, rows), rows)
+
+    def send(src, dst, sent, got, at, peer):
+        copy = pltpu.make_async_remote_copy(
+            src_ref=src,
+            dst_ref=dst,
+            send_sem=sent.at[at],
+            recv_sem=got.at[at],
+            device_id={"row": peer},
+            device_id_type=pl.DeviceIdType.MESH,
+        )
+        copy.start()
+        return copy
+
+    first = [
+        send(part_ref.at[span(peer)], terms_ref.at[d], sent1, got1, d, peer)
+        for d, peer in enumerate(peers)
+    ]
+    mine = part_ref[span(me)]
+    for d, copy in enumerate(first):
+        copy.wait_recv()
+        mine = mine + terms_ref[d]
+    total_ref[span(me)] = mine
+    second = [
+        send(total_ref.at[span(me)], total_ref.at[span(me)], sent2, got2, d, peer)
+        for d, peer in enumerate(peers)
+    ]
+    for copy in first:
+        copy.wait_send()
+    for copy in second:
+        copy.wait()
+    out_ref[...] = total_ref[...]
+
+
+def row_sum(part):
+    shards = lax.axis_size("row")
+    rows, width = part.shape
+    if shards == 1 or rows % (8 * shards):
+        return lax.psum(part, "row")
+    return pl.pallas_call(
+        lambda *refs: sum_kernel(shards, *refs),
+        out_shape=jax.ShapeDtypeStruct(part.shape, part.dtype),
+        in_specs=[pl.BlockSpec(memory_space=pltpu.VMEM)],
+        out_specs=pl.BlockSpec(memory_space=pltpu.VMEM),
+        scratch_shapes=[
+            pltpu.VMEM((shards - 1, rows // shards, width), part.dtype),
+            pltpu.VMEM(part.shape, part.dtype),
+        ]
+        + [pltpu.SemaphoreType.DMA((shards - 1,))] * 4,
+        compiler_params=pltpu.CompilerParams(
+            collective_id=0, has_side_effects=True, vmem_limit_bytes=8 * 2**20
+        ),
+        cost_estimate=pl.CostEstimate(
+            flops=part.size, bytes_accessed=4 * part.size * 4, transcendentals=0
+        ),
+    )(part)
+
+
 def body(features, blocks, block_ptr, block_col, held_out, weight, cotangent):
     shards = lax.axis_size("row")
     my_feat = lax.axis_index("feat")
@@ -185,9 +255,9 @@
     grad_part = lax.dot_general(
         piece, cotangent, (((0,), (0,)), ((), ())), preferred_element_type=f32
     )
-    grad_total = lax.psum(grad_part, "row")
+    grad_total = row_sum(grad_part)
+    returned, grad_total, layer_out = lax.optimization_barrier((returned, grad_total, layer_out))
     weight_grad = grad_total * (1.0 / jnp.sqrt(f32(rows_dev * shards)))
-
     feature_grad = local_call(
         collect_kernel,
         (asked,),

time: 295 us -> 234 us (0.79)
  waiting for transfers between devices: 199 us -> 95.5 us
  Pallas kernels: 18.7 us -> 64.9 us
    all_to_all x1, waiting for transfers between devices: 71.5 us -> 0.01 us  [body(): lax.all_to_all(sending, 'row', split_axis=0, concat_axis=0, tiled=True)]
    psum x1 -> x0, waiting for transfers between devices: 65.7 us -> none  [body(): grad_total = lax.psum(grad_part, 'row')]
    pallas_call x0 -> x1, Pallas kernels: none -> 46 us  [row_sum(): pl.pallas_call(lambda *refs: sum_kernel(shards, *refs), out_shape=jax.Sha...]
    all_gather x1, waiting for transfers between devices: 0.01 us -> 33.4 us  [body(): piece = lax.all_gather(aggregated, 'feat', axis=1, tiled=True)]
    unnamed x18 -> x20, local copies, waits for them, and re-layouts: 9.64 us -> 9.66 us
  transfers between devices with their start and end apart: 6 -> 5, of which waited for: 4 -> 3; matrix products, arithmetic and copies ran while one was open for 6% -> 8% of each run, Pallas kernels for 6% -> 25%
where the time goes in v2:
time: 234 us; the launch traced here: 233 us
  waiting for transfers between devices  95.5 us (41%)
  Pallas kernels  64.9 us (28%)
  blocking collectives  20.7 us (9%)
  between operations  13.9 us (6%)
  local copies, waits for them, and re-layouts  12.9 us (6%)
  starting transfers between devices  9.22 us (4%)
  matrix products  8.74 us (4%)
  other arithmetic  7.07 us (3%)
    pallas_call x1, Pallas kernels, row_sum(): pl.pallas_call(lambda *refs: sum_kernel(shards, *refs), out_shape=jax.Sha...  46 us
    all_to_all x1, waiting for transfers between devices, body(): lax.all_to_all(outgoing, 'row', split_axis=0, concat_axis=0, tiled=True)  35.3 us
    all_gather x1, waiting for transfers between devices, body(): piece = lax.all_gather(aggregated, 'feat', axis=1, tiled=True)  33.4 us
    all_gather x1, waiting for transfers between devices, body(): full_blocks = lax.all_gather(blocks, 'feat', axis=1, tiled=True)  25.3 us
    pallas_call x4, Pallas kernels, local_call(): pl.pallas_call(kernel, out_shape=out_shape, grid_spec=pltpu.PrefetchScala...  18.9 us
    all_to_all x1, blocking collectives, body(): lax.all_to_all(wanted, 'row', split_axis=0, concat_axis=0, tiled=True)  13.5 us
    unnamed x20, local copies, waits for them, and re-layouts  9.66 us
    all_gather x1, blocking collectives, body(): weight_piece = lax.all_gather(weight, 'feat', axis=1, tiled=True)  7.2 us
  transfers between devices with their start and end apart: 5, of which 3 were waited for; matrix products, arithmetic and copies ran while one was open for 8% of the time, Pallas kernels for 25%

profile of v2, /device:TPU:0, one launch (start us, length us, event | category | flops | bytes accessed | tf_op | source)
XLA Modules:
  0.0 232.9 jit_solution(3991974241135803277)
XLA Ops:
  7.2 0.0 all-gather.6.cloned.1.call-start
  7.2 0.7 all-gather.6.cloned.1.call-update
  7.9 1.2 slice.6
  9.1 0.6 iota_compare_fusion.3
  9.8 0.7 slice_bitcast_fusion
  10.5 0.1 convert_reduce_fusion.1
  10.6 1.3 fusion.5
  11.9 1.3 fusion.9
  13.2 0.2 convert_reduce_fusion
  13.4 1.3 fusion.7
  14.8 0.1 select_reduce_fusion
  14.9 0.1 sub.17
  15.0 13.5 %all_to_all.18 = s32[8,14,1]{1,2,0:T(1,128)S(1)} all-to-all(s32[8,14,1]{1,2,0:T(1,128)S(1)} %bitcast.37), channel_id=1, replica_groups=mesh['row'=8,'feat'=4] {'row'}, dimensions={0} | all-to-all | bytes 896 | tf_op jit(solution)/shard_map/all_to_all | solution.py:217
  28.5 0.5 broadcast.108
  29.0 0.7 reduce.3
  29.7 0.1 all_to_all.13.asked_ref
  29.8 0.0 copy-start.4
  29.8 1.2 copy-done.4
  31.0 0.0 copy-start.5
  31.0 0.7 copy-done.5
  31.6 1.9 shard_map.95
  33.5 0.0 copy-start
  33.5 1.9 copy-done
  35.5 0.0 copy-start.9
  35.5 4.6 %all-to-all-start.2 = ((bf16[112,128,128]{2,1,0:T(8,128)(2,1)}), bf16[112,128,128]{2,1,0:T(8,128)(2,1)}, u32[]{:S(2)}, u32[]{:S(2)}) async-start(bf16[112,128,128]{2,1,0:T(8,128)(2,1)} %copy-done), calls=%async_computation.2 | async-start | bytes 7340032 | tf_op jit(solution)/shard_map/all_to_all | solution.py:228
  40.1 0.0 all-gather.4.cloned.1.call-start
  40.1 0.7 all-gather.4.cloned.1.call-update
  40.8 0.0 copy-done.9
  40.9 7.2 %all_gather.13 = bf16[512,512]{1,0:T(8,128)(2,1)S(1)} all-gather(bf16[512,128]{1,0:T(8,128)(2,1)S(1)} %copy-done.9), channel_id=1, replica_groups=mesh['row'=8,'feat'=4] {'feat'}, dimensions={1}, use_global_device_ids=true | all-gather | bytes 655360 | tf_op jit(solution)/shard_map/all_gather | solution.py:231
  48.1 0.0 all-gather.6.cloned.1.call-done
  48.1 3.3 %fusion = bf16[3584,128]{0,1:T(8,128)(2,1)S(1)} fusion(bf16[3584,512]{1,0:T(8,128)(2,1)} %all-gather.6.cloned.1.call-done, bf16[512,512]{1,0:T(8,128)(2,1)S(1)} %all_gather.13, s32[]{:T(128)S(6)} %select_n.54), kind=kOutput, calls=%fused_computation.2 | convolution fusion | flops 470220800 | bytes 4718596 | tf_op jit(solution)/shard_map/dot_general | solution.py:233
  51.4 0.6 copy.13
  52.0 25.3 %all-gather.4.cloned.1.call-done.blocks_ref = bf16[112,128,128]{2,1,0:T(8,128)(2,1)} async-done(((bf16[112,32,128]{2,1,0:T(8,128)(2,1)}), bf16[112,128,128]{2,1,0:T(8,128)(2,1)}) %all-gather.4.cloned.1.call-update) | async-done | bytes 3670032 | tf_op jit(solution)/shard_map/all_gather | solution.py:219
  77.4 0.0 copy-start.2
  77.4 2.0 copy-done.2
  79.4 4.3 %shard_map.94 = bf16[112,128,128]{2,1,0:T(8,128)(2,1)S(1)} custom-call(s32[112]{0:T(128)S(1)} %get-tuple-element.11.slot_ref, s32[112]{0:T(128)S(1)} %get-tuple-element.10.brow_ref, bf16[112,128,128]{2,1,0:T(8,128)(2,1)S(1)} %copy-done.2, bf16[28,128,128]{2,1,0:T(8,128)(2,1)S(1)} %bitcast.34), custom_call_target="tpu_custom_call" | custom-call | flops 469762048 | bytes 8257536 | tf_op jit(solution)/shard_map/pallas_call | solution.py:14
  83.7 0.0 copy-start.1
  83.7 1.8 copy-done.1
  85.5 35.3 %all-to-all-done.2.arrived_ref = bf16[112,128,128]{2,1,0:T(8,128)(2,1)} async-done(((bf16[112,128,128]{2,1,0:T(8,128)(2,1)}), bf16[112,128,128]{2,1,0:T(8,128)(2,1)}, u32[]{:S(2)}, u32[]{:S(2)}) %all-to-all-start.2) | async-done | bytes 3670048 | tf_op jit(solution)/shard_map/all_to_all | solution.py:228
  120.9 4.5 %all-to-all-start = ((bf16[112,128,128]{2,1,0:T(8,128)(2,1)}), bf16[112,128,128]{2,1,0:T(8,128)(2,1)}, u32[]{:S(2)}, u32[]{:S(2)}) async-start(bf16[112,128,128]{2,1,0:T(8,128)(2,1)} %copy-done.1), calls=%async_computation | async-start | bytes 7340032 | tf_op jit(solution)/shard_map/all_to_all | solution.py:243
  125.4 0.0 all-gather.8.cloned.1.call-start
  125.4 0.7 select_maximum_fusion
  126.1 0.0 copy-start.3
  126.1 2.0 copy-done.3
  128.1 0.0 copy-start.8
  128.1 7.2 %shard_map.96 = bf16[28,128,128]{2,1,0:T(8,128)(2,1)} custom-call(s32[112]{0:T(128)S(1)} %get-tuple-element.16.position_ref, s32[112]{0:T(128)S(1)} %get-tuple-element.17.brow_ref, bf16[112,128,128]{2,1,0:T(8,128)(2,1)S(1)} %copy-done.3, bf16[112,128,128]{2,1,0:T(8,128)(2,1)} %all-to-all-done.2.arrived_ref), custom_call_target="tpu_custom_call" | custom-call | flops 469762048 | bytes 8257536 | tf_op jit(solution)/shard_map/pallas_call | solution.py:14
  135.3 0.0 all-gather.8.cloned.1.call-update
  135.3 33.4 %all-gather.8.cloned.1.call-done = bf16[3584,512]{1,0:T(8,128)(2,1)} async-done(((bf16[3584,128]{1,0:T(8,128)(2,1)}), bf16[3584,512]{1,0:T(8,128)(2,1)}) %all-gather.8.cloned.1.call-update) | async-done | bytes 3670032 | tf_op jit(solution)/shard_map/all_gather | solution.py:253
  168.7 0.0 copy-done.8
  168.7 0.0 copy-start.7
  168.7 3.4 %fusion.10.refs_0_ = f32[512,128]{1,0:T(8,128)S(1)} fusion(bf16[3584,512]{1,0:T(8,128)(2,1)} %all-gather.8.cloned.1.call-done, bf16[3584,128]{1,0:T(8,128)(2,1)S(1)} %copy-done.8), kind=kOutput, calls=%fused_computation.34 | convolution fusion | flops 469762048 | bytes 4849664 | tf_op jit(solution)/shard_map/dot_general | solution.py:255
  172.1 46.0 %shard_map.97 = f32[512,128]{1,0:T(8,128)S(1)} custom-call(f32[512,128]{1,0:T(8,128)S(1)} %fusion.10.refs_0_), custom_call_target="tpu_custom_call" | custom-call | flops 65536 | bytes 1048576 | tf_op jit(solution)/shard_map/pallas_call | solution.py:169
  218.1 0.0 copy-done.7
  218.1 0.0 copy-start.6
  218.1 2.0 convolution_convert_fusion
  220.1 0.0 all-to-all-done.returned_ref
  220.1 0.7 broadcast_multiply_fusion
  220.9 0.0 copy-done.6
  220.9 5.5 %shard_map.98 = bf16[28,128,128]{2,1,0:T(8,128)(2,1)} custom-call(s32[112]{0:T(128)S(1)} %all_to_all.13.asked_ref, s32[1,128]{1,0:T(1,128)S(1)} %copy-done.6, bf16[112,128,128]{2,1,0:T(8,128)(2,1)} %all-to-all-done.returned_ref), custom_call_target="tpu_custom_call" | custom-call | bytes 4588032 | tf_op jit(solution)/shard_map/pallas_call | solution.py:14
  (1 shorter events, 0.0 us)
Async XLA Ops:
  7.2 40.9 %all-gather.6.cloned.1.call-start = ((), (), s32[]{:S(2)}) async-start(), calls=%async_computation.4 | async-start | bytes 4587520 | tf_op jit(solution)/shard_map/all_gather | solution.py:230
  29.8 1.2 copy-start.4
  31.0 0.7 copy-start.5
  33.5 1.9 copy-start
  35.5 5.4 %copy-start.9 = (bf16[512,128]{1,0:T(8,128)(2,1)S(1)}, bf16[512,128]{1,0:T(8,128)(2,1)}, u32[]{:S(2)}) copy-start(bf16[512,128]{1,0:T(8,128)(2,1)} %param.12) | copy-start | bytes 393220
  35.5 85.4 %all-to-all-start.2 = ((bf16[112,128,128]{2,1,0:T(8,128)(2,1)}), bf16[112,128,128]{2,1,0:T(8,128)(2,1)}, u32[]{:S(2)}, u32[]{:S(2)}) async-start(bf16[112,128,128]{2,1,0:T(8,128)(2,1)} %copy-done), calls=%async_computation.2 | async-start | bytes 7340032 | tf_op jit(solution)/shard_map/all_to_all | solution.py:228
  40.1 37.3 %all-gather.4.cloned.1.call-start = ((), (), s32[]{:S(2)}) async-start(), calls=%async_computation.3 | async-start | bytes 4587520 | tf_op jit(solution)/shard_map/all_gather | solution.py:219
  77.4 2.0 copy-start.2
  83.7 1.8 copy-start.1
  120.9 99.3 %all-to-all-start = ((bf16[112,128,128]{2,1,0:T(8,128)(2,1)}), bf16[112,128,128]{2,1,0:T(8,128)(2,1)}, u32[]{:S(2)}, u32[]{:S(2)}) async-start(bf16[112,128,128]{2,1,0:T(8,128)(2,1)} %copy-done.1), calls=%async_computation | async-start | bytes 7340032 | tf_op jit(solution)/shard_map/all_to_all | solution.py:243
  125.4 43.3 %all-gather.8.cloned.1.call-start = ((), (), s32[]{:S(2)}) async-start(), calls=%async_computation.5 | async-start | bytes 4587520 | tf_op jit(solution)/shard_map/all_gather | solution.py:253
  126.1 2.0 copy-start.3
  128.1 40.6 %copy-start.8 = (bf16[3584,128]{1,0:T(8,128)(2,1)S(1)}, bf16[3584,128]{1,0:T(8,128)(2,1)}, u32[]{:S(2)}) copy-start(bf16[3584,128]{1,0:T(8,128)(2,1)} %param.13) | copy-start | bytes 2752516
  168.7 49.4 %copy-start.7 = (bf16[3584,512]{1,0:T(8,128)(2,1)S(1)}, bf16[3584,512]{1,0:T(8,128)(2,1)}, u32[]{:S(2)}) copy-start(bf16[3584,512]{1,0:T(8,128)(2,1)} %all-gather.8.cloned.1.call-done) | copy-start | bytes 11010052
  218.1 2.8 %copy-start.6 = (s32[1,128]{1,0:T(1,128)S(1)}, s32[1,128]{1,0:T(1,128)}, u32[]{:S(2)}) copy-start(s32[1,128]{1,0:T(1,128)} %held_ref.3) | copy-start | bytes 1540
Sparse Core Ops, SparseCore 0:
  9.5 34.8 all-gather.5
  46.0 31.3 all-gather.3
  135.4 33.2 all-gather.7

commit v3 on v2

--- a/solution.py
+++ b/solution.py
@@ -185,6 +185,176 @@
     )(part)
 
 
+def gather_kernel(
+    shards, meta_ref, held_ref, features_ref, out_ref, all_meta_ref,
+    kept_ref, meta_in_ref, own_sem, meta_sent, meta_got, line_sent, line_got, pair_sent, pair_got,
+):
+    block_rows, block_size, _ = features_ref.shape
+    places = shards // 2
+    me = lax.axis_index("row")
+    at, side = me // 2, lax.rem(me, 2)
+    other = 2 * at + 1 - side
+    late = max(1, block_rows // 7)
+    early = block_rows - late
+    cuts = [early * i // 3 for i in range(4)]
+    ranges = [pl.ds(a, b - a) for a, b in zip(cuts, cuts[1:])] + [pl.ds(early, late)]
+    last = len(ranges) - 1
+    streams = [(i, False) for i in range(len(ranges))] + [(last, True)]
+
+    barrier = pltpu.get_barrier_semaphore()
+    peers = [lax.rem(me + d, shards) for d in range(1, shards)]
+    for peer in peers:
+        pl.semaphore_signal(
+            barrier, inc=1, device_id={"row": peer}, device_id_type=pl.DeviceIdType.MESH
+        )
+
+    def keep(b, carry):
+        rows = features_ref[b].astype(jnp.float32)
+        hit = held_rows(held_ref, b, block_size)
+        kept_ref[b] = jnp.where(hit, 0.0, rows).astype(kept_ref.dtype)
+        return carry
+
+    lax.fori_loop(0, block_rows, keep, 0, unroll=4)
+    own = pltpu.make_async_copy(kept_ref, out_ref.at[me], own_sem)
+    own.start()
+    pl.semaphore_wait(barrier, shards - 1)
+
+    def remote(src, dst, sent, got, peer):
+        return pltpu.make_async_remote_copy(
+            src_ref=src,
+            dst_ref=dst,
+            send_sem=sent,
+            recv_sem=got,
+            device_id={"row": peer},
+            device_id_type=pl.DeviceIdType.MESH,
+        )
+
+    def piece(origin, part):
+        return out_ref.at[origin, ranges[part]]
+
+    def along(way, hop, n, origin_at):
+        part, crossed = streams[n]
+        origin = 2 * origin_at + (1 - side if crossed else side)
+        src = kept_ref.at[ranges[part]] if hop == 1 and not crossed else piece(origin, part)
+        k = (0 if way > 0 else 1, hop - 1, n)
+        return remote(src, piece(origin, part), line_sent.at[k], line_got.at[k], me + 2 * way)
+
+    def across(way, hop, part, origin_at):
+        origin = 2 * origin_at + side
+        src = kept_ref.at[ranges[part]] if hop == 0 else piece(origin, part)
+        k = (0 if way > 0 else 1, hop, part)
+        return remote(src, piece(origin, part), pair_sent.at[k], pair_got.at[k], other)
+
+    def ahead(way, hops=1):
+        return (at + way * hops >= 0) & (at + way * hops < places)
+
+    def start_line(way, n):
+        @pl.when(ahead(way))
+        def _():
+            along(way, 1, n, at).start()
+
+    order = [last] + list(range(last))
+    for part in order:
+        across(1, 0, part, at).start()
+        for way in (1, -1):
+            start_line(way, part)
+    metas = [
+        remote(meta_ref, meta_in_ref.at[me], meta_sent.at[d], meta_got.at[d], peer)
+        for d, peer in enumerate(peers)
+    ]
+    for copy in metas:
+        copy.start()
+    across(1, 0, last, at).wait_recv()
+    for way in (1, -1):
+        start_line(way, len(streams) - 1)
+
+    walk = [last] + list(range(last)) + [len(streams) - 1]
+    for hop in range(1, places):
+        for n in walk:
+            part, crossed = streams[n]
+            for way in (1, -1):
+
+                @pl.when(ahead(-way, hop))
+                def _():
+                    along(way, hop, n, at - way * hop).wait_recv()
+                    if part != last:
+                        across(way, hop, part, at - way * hop).start()
+                    if hop < places - 1:
+
+                        @pl.when(ahead(way))
+                        def _():
+                            along(way, hop + 1, n, at - way * hop).start()
+
+    for part in range(last):
+        across(1, 0, part, at).wait_recv()
+    for part in range(last + 1):
+        across(1, 0, part, at).wait_send()
+    for way in (1, -1):
+        for n in range(len(streams)):
+
+            @pl.when(ahead(way))
+            def _():
+                along(way, 1, n, at).wait_send()
+
+    for hop in range(1, places):
+        for way in (1, -1):
+
+            @pl.when(ahead(-way, hop))
+            def _():
+                for part in range(last):
+                    across(way, hop, part, at - way * hop).wait()
+                if hop < places - 1:
+
+                    @pl.when(ahead(way))
+                    def _():
+                        for n in range(len(streams)):
+                            along(way, hop + 1, n, at - way * hop).wait_send()
+
+    for copy in metas:
+        copy.wait()
+    own.wait()
+    all_meta_ref[...] = meta_in_ref[...]
+    all_meta_ref[me] = meta_ref[...]
+
+
+def gather_kept(meta, held_out, features, shards):
+    block_rows, block_size, width = features.shape
+    streams, places = 5, shards // 2
+    return pl.pallas_call(
+        lambda *refs: gather_kernel(shards, *refs),
+        out_shape=(
+            jax.ShapeDtypeStruct((shards, *features.shape), features.dtype),
+            jax.ShapeDtypeStruct((shards, *meta.shape), meta.dtype),
+        ),
+        in_specs=[pl.BlockSpec(memory_space=pltpu.VMEM)] * 3,
+        out_specs=(
+            pl.BlockSpec(memory_space=pl.ANY),
+            pl.BlockSpec(memory_space=pltpu.VMEM),
+        ),
+        scratch_shapes=[
+            pltpu.VMEM(features.shape, features.dtype),
+            pltpu.VMEM((shards, *meta.shape), meta.dtype),
+            pltpu.SemaphoreType.DMA,
+            pltpu.SemaphoreType.DMA((shards - 1,)),
+            pltpu.SemaphoreType.DMA((shards - 1,)),
+            pltpu.SemaphoreType.DMA((2, places, streams)),
+            pltpu.SemaphoreType.DMA((2, places, streams)),
+            pltpu.SemaphoreType.DMA((2, places, streams)),
+            pltpu.SemaphoreType.DMA((2, places, streams)),
+        ],
+        compiler_params=pltpu.CompilerParams(
+            collective_id=1, has_side_effects=True, vmem_limit_bytes=VMEM_LIMIT
+        ),
+        cost_estimate=pl.CostEstimate(
+            flops=0, bytes_accessed=30 * shards * features.size, transcendentals=0
+        ),
+    )(meta, held_out, features)
+
+
+def lane_pad(x):
+    return jnp.pad(x, ((0, 0), (0, -x.shape[1] % 128)))
+
+
 def body(features, blocks, block_ptr, block_col, held_out, weight, cotangent):
     shards = lax.axis_size("row")
     my_feat = lax.axis_index("feat")
@@ -214,21 +384,54 @@
     wanted = jnp.sum(match * (local[None, :] + 1), axis=1) - 1
     slot_at = jnp.sum(match * slots[None, :], axis=1)
     brow_at = jnp.sum(match * block_row[None, :], axis=1)
-    asked = lax.all_to_all(wanted, "row", split_axis=0, concat_axis=0, tiled=True)
-
+
+    block_shape = (block_size, width_dev)
+    feature_blocks = features.reshape(block_rows, *block_shape)
+    held = held_out
+    dense = jnp.concatenate([cotangent, weight], axis=0)
+    dense_piece = lax.all_gather(dense, "feat", axis=1, tiled=True)
     full_blocks = lax.all_gather(blocks, "feat", axis=1, tiled=True)
-    block_shape = (block_size, width_dev)
-    outgoing = local_call(
-        pack_kernel,
-        (asked,),
-        (held_out, features.reshape(block_rows, *block_shape)),
-        jax.ShapeDtypeStruct((buffer_len, *block_shape), bf16),
-        (pltpu.VMEM((block_rows, *block_shape), bf16),),
-    )
-    arrived = lax.all_to_all(outgoing, "row", split_axis=0, concat_axis=0, tiled=True)
-
-    cot_piece = lax.all_gather(cotangent, "feat", axis=1, tiled=True)
-    weight_piece = lax.all_gather(weight, "feat", axis=1, tiled=True)
+    whole = shards > 2 and shards % 2 == 0 and block_rows <= 2 * peer_cap
+    if whole:
+        span = max(block_rows + 1, slot_count)
+        tables = jnp.concatenate(
+            [
+                jnp.pad(block_ptr, ((0, 0), (0, span - block_rows - 1))),
+                jnp.pad(block_col, ((0, 0), (0, span - slot_count))),
+            ],
+            axis=0,
+        )
+        meta = lane_pad(jnp.pad(tables, ((0, 6), (0, 0))))
+        gathered, all_meta = gather_kept(meta, held, feature_blocks, shards)
+        gathered, dense_piece, full_blocks = lax.optimization_barrier(
+            (gathered, dense_piece, full_blocks)
+        )
+        me = lax.axis_index("row")
+        all_col = all_meta[:, 1, :slot_count]
+        all_live = slots[None, :] < all_meta[:, 0, block_rows][:, None]
+        named = all_live & (all_col // block_rows == me)
+        ahead = (slots[:, None] < slots[None, :]).astype(f32)
+        order = jnp.dot(named.astype(f32), ahead, preferred_element_type=f32).astype(jnp.int32)
+        at_rank = named[:, None, :] & (
+            order[:, None, :] == jnp.arange(peer_cap, dtype=jnp.int32)[None, :, None]
+        )
+        asked = jnp.sum(
+            jnp.where(at_rank, all_col[:, None, :] % block_rows + 1, 0), axis=2
+        ).reshape(buffer_len) - 1
+        arrived = gathered.reshape(shards * block_rows, *block_shape)
+        found = jnp.where(live, columns, 0)
+    else:
+        asked = lax.all_to_all(wanted, "row", split_axis=0, concat_axis=0, tiled=True)
+        outgoing = local_call(
+            pack_kernel,
+            (asked,),
+            (held, feature_blocks),
+            jax.ShapeDtypeStruct((buffer_len, *block_shape), bf16),
+            (pltpu.VMEM((block_rows, *block_shape), bf16),),
+        )
+        arrived = lax.all_to_all(outgoing, "row", split_axis=0, concat_axis=0, tiled=True)
+        found = jnp.maximum(position, 0)
+    cot_piece, weight_piece = dense_piece[:rows_dev], dense_piece[rows_dev:]
     weight_mine = lax.dynamic_slice_in_dim(weight_piece, my_feat * width_dev, width_dev, 0)
     agg_grad = lax.dot_general(
         cot_piece, weight_mine, (((1,), (1,)), ((), ())), preferred_element_type=f32
@@ -244,7 +447,7 @@
 
     aggregated = local_call(
         forward_kernel,
-        (jnp.maximum(position, 0), jnp.where(live, block_row, block_rows)),
+        (found, jnp.where(live, block_row, block_rows)),
         (full_blocks, arrived),
         jax.ShapeDtypeStruct((block_rows, *block_shape), bf16),
         (pltpu.VMEM((block_rows + 1, *block_shape), f32),),
@@ -261,7 +464,7 @@
     feature_grad = local_call(
         collect_kernel,
         (asked,),
-        (held_out, returned),
+        (held, returned),
         jax.ShapeDtypeStruct((block_rows, *block_shape), bf16),
         (pltpu.VMEM((block_rows + 1, *block_shape), f32),),
     ).reshape(rows_dev, width_dev)

time: 234 us -> 220 us (0.940)
  Pallas kernels: 64.9 us -> 138 us
  waiting for transfers between devices: 95.5 us -> 32.8 us
  blocking collectives: 20.7 us -> 0 us
  starting transfers between devices: 9.22 us -> 4.62 us
    pallas_call x0 -> x1, Pallas kernels: none -> 79.8 us  [gather_kept(): pl.pallas_call(lambda *refs: gather_kernel(shards, *refs), out_shape=(jax...]
    all_to_all x1 -> x0, waiting for transfers between devices: 35.3 us -> none  [body(): lax.all_to_all(outgoing, 'row', split_axis=0, concat_axis=0, tiled=True)]
    all_gather x1, waiting for transfers between devices: 25.3 us -> 0.02 us  [body(): full_blocks = lax.all_gather(blocks, 'feat', axis=1, tiled=True)]
    all_to_all x1 -> x0, blocking collectives: 13.5 us -> none  [body(): lax.all_to_all(wanted, 'row', split_axis=0, concat_axis=0, tiled=True)]
    all_gather x1 -> x0, blocking collectives: 7.2 us -> none  [body(): weight_piece = lax.all_gather(weight, 'feat', axis=1, tiled=True)]
    all_to_all x1 -> x0, starting transfers between devices: 4.62 us -> none  [body(): lax.all_to_all(outgoing, 'row', split_axis=0, concat_axis=0, tiled=True)]
    pallas_call x4 -> x3, Pallas kernels: 18.9 us -> 14.7 us  [local_call(): pl.pallas_call(kernel, out_shape=out_shape, grid_spec=pltpu.PrefetchScala...]
    pallas_call x1, Pallas kernels: 46 us -> 43 us  [row_sum(): pl.pallas_call(lambda *refs: sum_kernel(shards, *refs), out_shape=jax.Sha...]
  transfers between devices with their start and end apart: 5 -> 4, of which waited for: 3 -> 1; matrix products, arithmetic and copies ran while one was open for 8% -> 7% of each run, Pallas kernels for 25% -> 58%
where the time goes in v3:
time: 220 us; the launch traced here: 219 us
  Pallas kernels  138 us (63%)
  waiting for transfers between devices  32.8 us (15%)
  between operations  14 us (6%)
  local copies, waits for them, and re-layouts  12.1 us (6%)
  matrix products  10.8 us (5%)
  other arithmetic  7.48 us (3%)
  starting transfers between devices  4.62 us (2%)
    pallas_call x1, Pallas kernels, gather_kept(): pl.pallas_call(lambda *refs: gather_kernel(shards, *refs), out_shape=(jax...  79.8 us
    pallas_call x1, Pallas kernels, row_sum(): pl.pallas_call(lambda *refs: sum_kernel(shards, *refs), out_shape=jax.Sha...  43 us
    all_gather x1, waiting for transfers between devices, body(): piece = lax.all_gather(aggregated, 'feat', axis=1, tiled=True)  32 us
    pallas_call x3, Pallas kernels, local_call(): pl.pallas_call(kernel, out_shape=out_shape, grid_spec=pltpu.PrefetchScala...  14.7 us
    unnamed x22, local copies, waits for them, and re-layouts  9.94 us
    all_to_all x1, starting transfers between devices, body(): lax.all_to_all(sending, 'row', split_axis=0, concat_axis=0, tiled=True)  4.5 us
  transfers between devices with their start and end apart: 4, of which 1 were waited for; matrix products, arithmetic and copies ran while one was open for 7% of the time, Pallas kernels for 58%

profile of v3, /device:TPU:0, one launch (start us, length us, event | category | flops | bytes accessed | tf_op | source)
XLA Modules:
  0.0 219.3 jit_solution(1022257911367185286)
XLA Ops:
  7.2 0.0 copy-start.10
  7.2 0.0 copy-start.9
  7.2 0.0 copy-start.6
  7.2 0.0 copy-start.5
  7.2 0.0 all-gather.6.cloned.1.call-start
  7.2 0.7 all-gather.6.cloned.1.call-update
  7.9 0.0 all-gather.4.cloned.1.call-start
  8.0 2.3 %pad_maximum_fusion = bf16[4096,128]{1,0:T(8,128)(2,1)} fusion(bf16[512,128]{1,0:T(8,128)(2,1)} %param.12, bf16[3584,128]{1,0:T(8,128)(2,1)} %param.13), kind=kLoop, calls=%fused_computation.4 | loop fusion | flops 2097152 | bytes 2097152 | tf_op jit(solution)/shard_map/concatenate | solution.py:391
  10.3 0.0 all-gather.4.cloned.1.call-update
  10.3 0.0 copy-done.10
  10.3 0.6 slice.18
  10.9 0.0 copy-done.9
  10.9 0.0 copy-done.6
  11.0 0.0 copy-done.5
  11.0 79.8 %shard_map.94 = (bf16[8,28,128,128]{3,2,1,0:T(8,128)(2,1)S(1)}, s32[8,8,128]{2,1,0:T(8,128)S(1)}) custom-call(s32[8,128]{1,0:T(8,128)S(1)} %pad.20.refs_0_, s32[1,128]{1,0:T(1,128)S(1)} %copy-done.6, bf16[28,128,128]{2,1,0:T(8,128)(2,1)S(1)} %bitcast.48), custom_call_target="tpu_custom_call" | custom-call | bytes 110100480 | tf_op jit(solution)/shard_map/pallas_call | solution.py:323
  90.8 0.0 copy-start.3
  90.8 3.0 %copy-done.3 = bf16[8,28,128,128]{3,2,1,0:T(8,128)(2,1)} copy-done((bf16[8,28,128,128]{3,2,1,0:T(8,128)(2,1)}, bf16[8,28,128,128]{3,2,1,0:T(8,128)(2,1)S(1)}, u32[]{:S(2)}) %copy-start.3) | copy-done | bytes 7340056
  93.8 0.6 iota_compare_fusion.8
  94.5 0.1 slice_bitcast_fusion
  94.6 0.1 convert_reduce_fusion.1
  94.7 0.7 fusion.28
  95.3 0.7 bitcast_select_fusion
  96.0 0.2 convert_reduce_fusion
  96.2 0.7 fusion.18
  96.8 0.1 select_reduce_fusion.1
  96.9 0.0 all-gather.6.cloned.1.call-done.blocks_ref
  97.0 0.0 all-gather.4.cloned.1.call-done
  97.0 1.1 slice.21
  98.1 0.0 copy-start.1
  98.1 3.3 %convolution_convert_fusion.1 = bf16[3584,128]{1,0:T(8,128)(2,1)S(1)} fusion(bf16[4096,512]{1,0:T(8,128)(2,1)} %all-gather.4.cloned.1.call-done, bf16[512,512]{1,0:T(8,128)(2,1)S(1)} %slice.21, s32[]{:T(128)S(6)} %select_n.62), kind=kOutput, calls=%fused_computation.1 | convolution fusion | flops 470220800 | bytes 4718596 | tf_op jit(solution)/shard_map/dot_general | solution.py:436
  101.4 0.0 copy-done.1
  101.4 4.2 %shard_map.95 = bf16[112,128,128]{2,1,0:T(8,128)(2,1)S(1)} custom-call(s32[112]{0:T(128)S(1)} %get-tuple-element.20.slot_ref, s32[112]{0:T(128)S(1)} %get-tuple-element.19.brow_ref, bf16[112,128,128]{2,1,0:T(8,128)(2,1)S(1)} %copy-done.1, bf16[28,128,128]{2,1,0:T(8,128)(2,1)S(1)} %bitcast.47), custom_call_target="tpu_custom_call" | custom-call | flops 469762048 | bytes 8257536 | tf_op jit(solution)/shard_map/pallas_call | solution.py:14
  105.6 0.0 copy-start
  105.6 1.8 copy-done
  107.4 4.5 %all-to-all-start = ((bf16[112,128,128]{2,1,0:T(8,128)(2,1)}), bf16[112,128,128]{2,1,0:T(8,128)(2,1)}, u32[]{:S(2)}, u32[]{:S(2)}) async-start(bf16[112,128,128]{2,1,0:T(8,128)(2,1)} %copy-done), calls=%async_computation | async-start | bytes 7340032 | tf_op jit(solution)/shard_map/all_to_all | solution.py:446
  111.9 0.0 all-gather.8.cloned.1.call-start
  112.0 0.7 broadcast_select_fusion.brow_ref
  112.6 0.0 copy-start.2
  112.6 2.0 copy-done.2
  114.7 0.0 copy-start.4
  114.7 3.1 %copy-done.4 = bf16[8,28,128,128]{3,2,1,0:T(8,128)(2,1)S(1)} copy-done((bf16[8,28,128,128]{3,2,1,0:T(8,128)(2,1)S(1)}, bf16[8,28,128,128]{3,2,1,0:T(8,128)(2,1)}, u32[]{:S(2)}) %copy-start.4) | copy-done | bytes 7340056
  117.7 0.0 copy-start.7
  117.7 5.0 %shard_map.96 = bf16[28,128,128]{2,1,0:T(8,128)(2,1)} custom-call(s32[112]{0:T(128)S(1)} %get-tuple-element.25.position_ref, s32[112]{0:T(128)S(1)} %broadcast_select_fusion.brow_ref, bf16[112,128,128]{2,1,0:T(8,128)(2,1)S(1)} %copy-done.2, bf16[224,128,128]{2,1,0:T(8,128)(2,1)S(1)} %bitcast.46), custom_call_target="tpu_custom_call" | custom-call | flops 469762048 | bytes 11927552 | tf_op jit(solution)/shard_map/pallas_call | solution.py:14
  122.8 0.0 copy-start.8
  122.8 0.0 all-gather.8.cloned.1.call-update
  122.8 0.3 slice_reduce_fusion
  123.1 0.4 slice_divide_fusion
  123.5 0.1 fusion.9
  123.6 0.2 convolution_convert_fusion.2
  123.8 0.3 select_reduce_fusion
  124.1 0.1 copy.31
  124.2 32.0 %all-gather.8.cloned.1.call-done = bf16[3584,512]{1,0:T(8,128)(2,1)} async-done(((bf16[3584,128]{1,0:T(8,128)(2,1)}), bf16[3584,512]{1,0:T(8,128)(2,1)}) %all-gather.8.cloned.1.call-update) | async-done | bytes 3670032 | tf_op jit(solution)/shard_map/all_gather | solution.py:456
  156.2 0.0 copy-done.7
  156.2 3.2 %fusion.23.refs_0_ = f32[512,128]{1,0:T(8,128)S(1)} fusion(bf16[3584,512]{1,0:T(8,128)(2,1)} %all-gather.8.cloned.1.call-done, bf16[3584,128]{1,0:T(8,128)(2,1)S(1)} %copy-done.7), kind=kOutput, calls=%fused_computation.57 | convolution fusion | flops 469762048 | bytes 4849664 | tf_op jit(solution)/shard_map/dot_general | solution.py:458
  159.4 0.1 sub.27.asked_ref
  159.5 43.0 %shard_map.97 = f32[512,128]{1,0:T(8,128)S(1)} custom-call(f32[512,128]{1,0:T(8,128)S(1)} %fusion.23.refs_0_), custom_call_target="tpu_custom_call" | custom-call | flops 65536 | bytes 1048576 | tf_op jit(solution)/shard_map/pallas_call | solution.py:169
  202.5 0.0 copy-done.8
  202.5 4.1 %convolution_convert_fusion = bf16[3584,128]{1,0:T(8,128)(2,1)} fusion(bf16[3584,512]{1,0:T(8,128)(2,1)} %all-gather.8.cloned.1.call-done, bf16[512,128]{1,0:T(8,128)(2,1)S(1)} %copy-done.8), kind=kOutput, calls=%fused_computation | convolution fusion | flops 470220800 | bytes 4718592 | tf_op jit(solution)/shard_map/dot_general | solution.py:457
  206.6 0.0 all-to-all-done.returned_ref
  206.6 0.7 broadcast_multiply_fusion
  207.3 5.5 %shard_map.98 = bf16[28,128,128]{2,1,0:T(8,128)(2,1)} custom-call(s32[112]{0:T(128)S(1)} %sub.27.asked_ref, s32[1,128]{1,0:T(1,128)S(1)} %copy-done.6, bf16[112,128,128]{2,1,0:T(8,128)(2,1)} %all-to-all-done.returned_ref), custom_call_target="tpu_custom_call" | custom-call | bytes 4588032 | tf_op jit(solution)/shard_map/pallas_call | solution.py:14
  (5 shorter events, 0.0 us)
Async XLA Ops:
  7.2 3.2 %copy-start.10 = (s32[1,29]{1,0:T(1,128)S(1)}, s32[1,29]{1,0:T(1,128)}, u32[]{:S(2)}) copy-start(s32[1,29]{1,0:T(1,128)} %param.9) | copy-start | bytes 352
  7.2 3.7 %copy-start.9 = (s32[1,112]{1,0:T(1,128)S(1)}, s32[1,112]{1,0:T(1,128)}, u32[]{:S(2)}) copy-start(s32[1,112]{1,0:T(1,128)} %param.10) | copy-start | bytes 1348
  7.2 3.8 %copy-start.6 = (s32[1,128]{1,0:T(1,128)S(1)}, s32[1,128]{1,0:T(1,128)}, u32[]{:S(2)}) copy-start(s32[1,128]{1,0:T(1,128)} %held_ref.1) | copy-start | bytes 1540
  7.2 3.8 %copy-start.5 = (bf16[3584,128]{1,0:T(8,128)(2,1)S(1)}, bf16[3584,128]{1,0:T(8,128)(2,1)}, u32[]{:S(2)}) copy-start(bf16[3584,128]{1,0:T(8,128)(2,1)} %param.7) | copy-start | bytes 2752516
  7.2 89.8 %all-gather.6.cloned.1.call-start = ((), (), s32[]{:S(2)}) async-start(), calls=%async_computation.2 | async-start | bytes 4587520 | tf_op jit(solution)/shard_map/all_gather | solution.py:393
  7.9 89.1 %all-gather.4.cloned.1.call-start = ((), (), s32[]{:S(2)}) async-start(), calls=%async_computation.1 | async-start | bytes 5242880 | tf_op jit(solution)/shard_map/all_gather | solution.py:392
  90.8 3.0 %copy-start.3 = (bf16[8,28,128,128]{3,2,1,0:T(8,128)(2,1)}, bf16[8,28,128,128]{3,2,1,0:T(8,128)(2,1)S(1)}, u32[]{:S(2)}) copy-start(bf16[8,28,128,128]{3,2,1,0:T(8,128)(2,1)S(1)} %get-tuple-element.14) | copy-start | bytes 22020100
  98.1 3.3 %copy-start.1 = (bf16[112,128,128]{2,1,0:T(8,128)(2,1)S(1)}, bf16[112,128,128]{2,1,0:T(8,128)(2,1)}, u32[]{:S(2)}) copy-start(bf16[112,128,128]{2,1,0:T(8,128)(2,1)} %all-gather.6.cloned.1.call-done.blocks_ref) | copy-start | bytes 11010052
  105.6 1.8 copy-start
  107.4 99.2 %all-to-all-start = ((bf16[112,128,128]{2,1,0:T(8,128)(2,1)}), bf16[112,128,128]{2,1,0:T(8,128)(2,1)}, u32[]{:S(2)}, u32[]{:S(2)}) async-start(bf16[112,128,128]{2,1,0:T(8,128)(2,1)} %copy-done), calls=%async_computation | async-start | bytes 7340032 | tf_op jit(solution)/shard_map/all_to_all | solution.py:446
  111.9 44.3 %all-gather.8.cloned.1.call-start = ((), (), s32[]{:S(2)}) async-start(), calls=%async_computation.3 | async-start | bytes 4587520 | tf_op jit(solution)/shard_map/all_gather | solution.py:456
  112.6 2.0 copy-start.2
  114.7 3.1 %copy-start.4 = (bf16[8,28,128,128]{3,2,1,0:T(8,128)(2,1)S(1)}, bf16[8,28,128,128]{3,2,1,0:T(8,128)(2,1)}, u32[]{:S(2)}) copy-start(bf16[8,28,128,128]{3,2,1,0:T(8,128)(2,1)} %copy-done.3) | copy-start | bytes 22020100
  117.7 38.4 %copy-start.7 = (bf16[3584,128]{1,0:T(8,128)(2,1)S(1)}, bf16[3584,128]{1,0:T(8,128)(2,1)}, u32[]{:S(2)}) copy-start(bf16[3584,128]{1,0:T(8,128)(2,1)} %param.13) | copy-start | bytes 2752516
  122.8 79.7 %copy-start.8 = (bf16[512,128]{1,0:T(8,128)(2,1)S(1)}, bf16[512,128]{1,0:T(8,128)(2,1)}, u32[]{:S(2)}) copy-start(bf16[512,128]{1,0:T(8,128)(2,1)} %param.12) | copy-start | bytes 393220
Sparse Core Ops, SparseCore 0:
  9.6 34.1 all-gather.5
  45.4 35.0 all-gather.3
  122.9 33.2 all-gather.7

commit v4 on v3

--- a/solution.py
+++ b/solution.py
@@ -5,7 +5,7 @@
 from jax.experimental.pallas import tpu as pltpu
 from jax.sharding import PartitionSpec as P
 
-VMEM_LIMIT = 40 * 2**20
+VMEM_LIMIT = 58 * 2**20
 
 
 def local_call(kernel, scalars, operands, out_shape, scratch=(), flops=0):
@@ -403,8 +403,8 @@
         )
         meta = lane_pad(jnp.pad(tables, ((0, 6), (0, 0))))
         gathered, all_meta = gather_kept(meta, held, feature_blocks, shards)
-        gathered, dense_piece, full_blocks = lax.optimization_barrier(
-            (gathered, dense_piece, full_blocks)
+        all_meta, dense_piece, full_blocks = lax.optimization_barrier(
+            (all_meta, dense_piece, full_blocks)
         )
         me = lax.axis_index("row")
         all_col = all_meta[:, 1, :slot_count]
@@ -458,8 +458,9 @@
     grad_part = lax.dot_general(
         piece, cotangent, (((0,), (0,)), ((), ())), preferred_element_type=f32
     )
+    grad_part, layer_out = lax.optimization_barrier((grad_part, layer_out))
     grad_total = row_sum(grad_part)
-    returned, grad_total, layer_out = lax.optimization_barrier((returned, grad_total, layer_out))
+    returned, grad_total = lax.optimization_barrier((returned, grad_total))
     weight_grad = grad_total * (1.0 / jnp.sqrt(f32(rows_dev * shards)))
     feature_grad = local_call(
         collect_kernel,

time: 220 us -> 220 us (level)
  Pallas kernels: 138 us -> 147 us
  local copies, waits for them, and re-layouts: 12.1 us -> 4.2 us
  other arithmetic: 7.48 us -> 9.86 us
    unnamed x22 -> x10, local copies, waits for them, and re-layouts: 9.94 us -> 0.02 us
    pallas_call x3, Pallas kernels: 14.7 us -> 23.6 us  [local_call(): pl.pallas_call(kernel, out_shape=out_shape, grid_spec=pltpu.PrefetchScala...]
  transfers between devices with their start and end apart: 4 -> 4, of which waited for: 1 -> 1; matrix products, arithmetic and copies ran while one was open for 7% -> 8% of each run, Pallas kernels for 58% -> 60%
where the time goes in v4:
time: 220 us; the launch traced here: 219 us
  Pallas kernels  147 us (67%)
  waiting for transfers between devices  30.6 us (14%)
  between operations  13.9 us (6%)
  other arithmetic  9.86 us (4%)
  matrix products  9.66 us (4%)
  starting transfers between devices  4.64 us (2%)
  local copies, waits for them, and re-layouts  4.2 us (2%)
    pallas_call x1, Pallas kernels, gather_kept(): pl.pallas_call(lambda *refs: gather_kernel(shards, *refs), out_shape=(jax...  82 us
    pallas_call x1, Pallas kernels, row_sum(): pl.pallas_call(lambda *refs: sum_kernel(shards, *refs), out_shape=jax.Sha...  40.9 us
    all_gather x1, waiting for transfers between devices, body(): piece = lax.all_gather(aggregated, 'feat', axis=1, tiled=True)  29.9 us
    pallas_call x3, Pallas kernels, local_call(): pl.pallas_call(kernel, out_shape=out_shape, grid_spec=pltpu.PrefetchScala...  23.6 us
    all_to_all x1, starting transfers between devices, body(): lax.all_to_all(sending, 'row', split_axis=0, concat_axis=0, tiled=True)  4.52 us
  transfers between devices with their start and end apart: 4, of which 1 were waited for; matrix products, arithmetic and copies ran while one was open for 8% of the time, Pallas kernels for 60%

profile of v4, /device:TPU:0, one launch (start us, length us, event | category | flops | bytes accessed | tf_op | source)
XLA Modules:
  0.0 219.3 jit_solution(4431072380380714714)
XLA Ops:
  7.2 0.0 copy-start.4
  7.2 0.0 copy-start.3
  7.2 0.0 all-gather.6.cloned.1.call-start
  7.2 0.7 all-gather.6.cloned.1.call-update
  7.9 0.0 all-gather.4.cloned.1.call-start
  8.0 2.3 %pad_maximum_fusion = bf16[4096,128]{1,0:T(8,128)(2,1)} fusion(bf16[512,128]{1,0:T(8,128)(2,1)} %param.12, bf16[3584,128]{1,0:T(8,128)(2,1)} %param.13), kind=kLoop, calls=%fused_computation.4 | loop fusion | flops 2097152 | bytes 2097152 | tf_op jit(solution)/shard_map/concatenate | solution.py:391
  10.3 0.0 all-gather.4.cloned.1.call-update
  10.3 0.0 copy-done.4
  10.3 0.6 slice.18
  10.9 0.0 copy-done.3
  10.9 0.6 pad.20.refs_0_
  11.5 82.0 %shard_map.94 = (bf16[8,28,128,128]{3,2,1,0:T(8,128)(2,1)}, s32[8,8,128]{2,1,0:T(8,128)}) custom-call(s32[8,128]{1,0:T(8,128)} %pad.20.refs_0_, s32[1,128]{1,0:T(1,128)} %held_ref.1, bf16[28,128,128]{2,1,0:T(8,128)(2,1)} %bitcast.50), custom_call_target="tpu_custom_call" | custom-call | bytes 110100480 | tf_op jit(solution)/shard_map/pallas_call | solution.py:323
  93.5 0.7 iota_compare_fusion.8
  94.2 0.1 slice_bitcast_fusion
  94.2 0.1 convert_reduce_fusion.1
  94.3 0.7 fusion.28
  95.0 1.2 fusion.19
  96.1 0.2 convert_reduce_fusion
  96.3 0.7 fusion.18
  97.0 0.7 select_reduce_fusion
  97.6 0.0 all-gather.6.cloned.1.call-done.blocks_ref
  97.6 0.0 all-gather.4.cloned.1.call-done
  97.6 1.1 slice.23
  98.7 4.1 %convolution_convert_fusion = bf16[3584,128]{1,0:T(8,128)(2,1)} fusion(bf16[4096,512]{1,0:T(8,128)(2,1)} %all-gather.4.cloned.1.call-done, bf16[512,512]{1,0:T(8,128)(2,1)S(1)} %slice.23, s32[]{:T(128)S(6)} %select_n.68), kind=kOutput, calls=%fused_computation | convolution fusion | flops 470220800 | bytes 4718596 | tf_op jit(solution)/shard_map/dot_general | solution.py:436
  102.8 8.5 %shard_map.96 = bf16[112,128,128]{2,1,0:T(8,128)(2,1)} custom-call(s32[112]{0:T(128)} %get-tuple-element.22.slot_ref, s32[112]{0:T(128)} %get-tuple-element.21.brow_ref, bf16[112,128,128]{2,1,0:T(8,128)(2,1)} %all-gather.6.cloned.1.call-done.blocks_ref, bf16[28,128,128]{2,1,0:T(8,128)(2,1)} %bitcast.48), custom_call_target="tpu_custom_call" | custom-call | flops 469762048 | bytes 8257536 | tf_op jit(solution)/shard_map/pallas_call | solution.py:14
  111.3 4.5 %all-to-all-start = ((bf16[112,128,128]{2,1,0:T(8,128)(2,1)}), bf16[112,128,128]{2,1,0:T(8,128)(2,1)}, u32[]{:S(2)}, u32[]{:S(2)}) async-start(bf16[112,128,128]{2,1,0:T(8,128)(2,1)} %shard_map.96), calls=%async_computation | async-start | bytes 7340032 | tf_op jit(solution)/shard_map/all_to_all | solution.py:446
  115.9 0.0 all-gather.8.cloned.1.call-start
  115.9 1.2 broadcast_select_fusion.brow_ref
  117.1 0.0 copy-start.2
  117.1 9.5 %shard_map.95 = bf16[28,128,128]{2,1,0:T(8,128)(2,1)} custom-call(s32[112]{0:T(128)} %get-tuple-element.28.position_ref, s32[112]{0:T(128)} %broadcast_select_fusion.brow_ref, bf16[112,128,128]{2,1,0:T(8,128)(2,1)} %all-gather.6.cloned.1.call-done.blocks_ref, bf16[224,128,128]{2,1,0:T(8,128)(2,1)} %bitcast.46), custom_call_target="tpu_custom_call" | custom-call | flops 469762048 | bytes 11927552 | tf_op jit(solution)/shard_map/pallas_call | solution.py:14
  126.6 0.0 copy-start.1
  126.6 0.0 all-gather.8.cloned.1.call-update
  126.6 1.1 slice_reduce_fusion
  127.8 1.1 slice_divide_fusion
  128.9 0.1 fusion.9
  129.0 0.2 convolution_convert_fusion.2
  129.2 0.3 select_reduce_fusion.2
  129.5 0.1 copy.31
  129.6 0.6 sub.25.asked_ref
  130.2 29.9 %all-gather.8.cloned.1.call-done = bf16[3584,512]{1,0:T(8,128)(2,1)} async-done(((bf16[3584,128]{1,0:T(8,128)(2,1)}), bf16[3584,512]{1,0:T(8,128)(2,1)}) %all-gather.8.cloned.1.call-update) | async-done | bytes 3670032 | tf_op jit(solution)/shard_map/all_gather | solution.py:456
  160.1 0.0 copy-done.2
  160.1 0.0 copy-start
  160.1 4.2 %convolution_convert_fusion.1 = bf16[3584,128]{1,0:T(8,128)(2,1)} fusion(bf16[3584,512]{1,0:T(8,128)(2,1)} %all-gather.8.cloned.1.call-done, bf16[512,128]{1,0:T(8,128)(2,1)S(1)} %copy-done.2), kind=kOutput, calls=%fused_computation.1 | convolution fusion | flops 470220800 | bytes 4718592 | tf_op jit(solution)/shard_map/dot_general | solution.py:457
  164.3 0.0 copy-done.1
  164.3 0.0 copy-done
  164.3 1.2 fusion.23.refs_0_
  165.5 40.9 %shard_map.97 = f32[512,128]{1,0:T(8,128)S(1)} custom-call(f32[512,128]{1,0:T(8,128)S(1)} %fusion.23.refs_0_), custom_call_target="tpu_custom_call" | custom-call | flops 65536 | bytes 1048576 | tf_op jit(solution)/shard_map/pallas_call | solution.py:169
  206.4 0.0 all-to-all-done.returned_ref
  206.4 0.7 broadcast_multiply_fusion
  207.2 5.6 %shard_map.98 = bf16[28,128,128]{2,1,0:T(8,128)(2,1)} custom-call(s32[112]{0:T(128)} %sub.25.asked_ref, s32[1,128]{1,0:T(1,128)} %held_ref.1, bf16[112,128,128]{2,1,0:T(8,128)(2,1)} %all-to-all-done.returned_ref), custom_call_target="tpu_custom_call" | custom-call | bytes 4588032 | tf_op jit(solution)/shard_map/pallas_call | solution.py:14
  (4 shorter events, 0.0 us)
Async XLA Ops:
  7.2 3.1 %copy-start.4 = (s32[1,29]{1,0:T(1,128)S(1)}, s32[1,29]{1,0:T(1,128)}, u32[]{:S(2)}) copy-start(s32[1,29]{1,0:T(1,128)} %param.9) | copy-start | bytes 352
  7.2 3.7 %copy-start.3 = (s32[1,112]{1,0:T(1,128)S(1)}, s32[1,112]{1,0:T(1,128)}, u32[]{:S(2)}) copy-start(s32[1,112]{1,0:T(1,128)} %param.10) | copy-start | bytes 1348
  7.2 90.5 %all-gather.6.cloned.1.call-start = ((), (), s32[]{:S(2)}) async-start(), calls=%async_computation.2 | async-start | bytes 4587520 | tf_op jit(solution)/shard_map/all_gather | solution.py:393
  7.9 89.7 %all-gather.4.cloned.1.call-start = ((), (), s32[]{:S(2)}) async-start(), calls=%async_computation.1 | async-start | bytes 5242880 | tf_op jit(solution)/shard_map/all_gather | solution.py:392
  111.3 95.1 %all-to-all-start = ((bf16[112,128,128]{2,1,0:T(8,128)(2,1)}), bf16[112,128,128]{2,1,0:T(8,128)(2,1)}, u32[]{:S(2)}, u32[]{:S(2)}) async-start(bf16[112,128,128]{2,1,0:T(8,128)(2,1)} %shard_map.96), calls=%async_computation | async-start | bytes 7340032 | tf_op jit(solution)/shard_map/all_to_all | solution.py:446
  115.9 44.2 %all-gather.8.cloned.1.call-start = ((), (), s32[]{:S(2)}) async-start(), calls=%async_computation.3 | async-start | bytes 4587520 | tf_op jit(solution)/shard_map/all_gather | solution.py:456
  117.1 42.9 %copy-start.2 = (bf16[512,128]{1,0:T(8,128)(2,1)S(1)}, bf16[512,128]{1,0:T(8,128)(2,1)}, u32[]{:S(2)}) copy-start(bf16[512,128]{1,0:T(8,128)(2,1)} %param.12) | copy-start | bytes 393220
  126.6 37.7 %copy-start.1 = (bf16[3584,128]{1,0:T(8,128)(2,1)S(1)}, bf16[3584,128]{1,0:T(8,128)(2,1)}, u32[]{:S(2)}) copy-start(bf16[3584,128]{1,0:T(8,128)(2,1)} %param.13) | copy-start | bytes 2752516
  160.1 4.2 %copy-start = (bf16[3584,512]{1,0:T(8,128)(2,1)S(1)}, bf16[3584,512]{1,0:T(8,128)(2,1)}, u32[]{:S(2)}) copy-start(bf16[3584,512]{1,0:T(8,128)(2,1)} %all-gather.8.cloned.1.call-done) | copy-start | bytes 11010052
Sparse Core Ops, SparseCore 0:
  9.6 34.1 all-gather.5
  45.4 35.0 all-gather.3
  126.7 33.2 all-gather.7

commit v5 on v4

--- a/solution.py
+++ b/solution.py
@@ -214,10 +214,7 @@
         kept_ref[b] = jnp.where(hit, 0.0, rows).astype(kept_ref.dtype)
         return carry
 
-    lax.fori_loop(0, block_rows, keep, 0, unroll=4)
     own = pltpu.make_async_copy(kept_ref, out_ref.at[me], own_sem)
-    own.start()
-    pl.semaphore_wait(barrier, shards - 1)
 
     def remote(src, dst, sent, got, peer):
         return pltpu.make_async_remote_copy(
@@ -255,6 +252,10 @@
 
     order = [last] + list(range(last))
     for part in order:
+        first = early if part == last else cuts[part]
+        lax.fori_loop(first, first + ranges[part].size, keep, 0)
+        if part == last:
+            pl.semaphore_wait(barrier, shards - 1)
         across(1, 0, part, at).start()
         for way in (1, -1):
             start_line(way, part)
@@ -264,6 +265,7 @@
     ]
     for copy in metas:
         copy.start()
+    own.start()
     across(1, 0, last, at).wait_recv()
     for way in (1, -1):
         start_line(way, len(streams) - 1)

time: 220 us -> 220 us (level)
  no operation moved by 1% of the time
where the time goes in v5:
time: 220 us; the launch traced here: 219 us
  Pallas kernels  147 us (67%)
  waiting for transfers between devices  30.6 us (14%)
  between operations  13.9 us (6%)
  other arithmetic  9.86 us (4%)
  matrix products  9.66 us (4%)
  starting transfers between devices  4.64 us (2%)
  local copies, waits for them, and re-layouts  4.2 us (2%)
    pallas_call x1, Pallas kernels, gather_kept(): pl.pallas_call(lambda *refs: gather_kernel(shards, *refs), out_shape=(jax...  82 us
    pallas_call x1, Pallas kernels, row_sum(): pl.pallas_call(lambda *refs: sum_kernel(shards, *refs), out_shape=jax.Sha...  40.9 us
    all_gather x1, waiting for transfers between devices, body(): piece = lax.all_gather(aggregated, 'feat', axis=1, tiled=True)  29.9 us
    pallas_call x3, Pallas kernels, local_call(): pl.pallas_call(kernel, out_shape=out_shape, grid_spec=pltpu.PrefetchScala...  23.6 us
    all_to_all x1, starting transfers between devices, body(): lax.all_to_all(sending, 'row', split_axis=0, concat_axis=0, tiled=True)  4.52 us
  transfers between devices with their start and end apart: 4, of which 1 were waited for; matrix products, arithmetic and copies ran while one was open for 8% of the time, Pallas kernels for 60%

profile of v5, /device:TPU:0, one launch (start us, length us, event | category | flops | bytes accessed | tf_op | source)
XLA Modules:
  0.0 219.3 jit_solution(11614632483091691290)
XLA Ops:
  7.2 0.0 copy-start.4
  7.2 0.0 copy-start.3
  7.2 0.0 all-gather.6.cloned.1.call-start
  7.2 0.7 all-gather.6.cloned.1.call-update
  7.9 0.0 all-gather.4.cloned.1.call-start
  8.0 2.3 %pad_maximum_fusion = bf16[4096,128]{1,0:T(8,128)(2,1)} fusion(bf16[512,128]{1,0:T(8,128)(2,1)} %param.12, bf16[3584,128]{1,0:T(8,128)(2,1)} %param.13), kind=kLoop, calls=%fused_computation.4 | loop fusion | flops 2097152 | bytes 2097152 | tf_op jit(solution)/shard_map/concatenate | solution.py:393
  10.3 0.0 all-gather.4.cloned.1.call-update
  10.3 0.0 copy-done.4
  10.3 0.6 slice.18
  10.9 0.0 copy-done.3
  10.9 0.6 pad.20.refs_0_
  11.5 82.0 %shard_map.94 = (bf16[8,28,128,128]{3,2,1,0:T(8,128)(2,1)}, s32[8,8,128]{2,1,0:T(8,128)}) custom-call(s32[8,128]{1,0:T(8,128)} %pad.20.refs_0_, s32[1,128]{1,0:T(1,128)} %held_ref.1, bf16[28,128,128]{2,1,0:T(8,128)(2,1)} %bitcast.50), custom_call_target="tpu_custom_call" | custom-call | bytes 110100480 | tf_op jit(solution)/shard_map/pallas_call | solution.py:325
  93.5 0.7 iota_compare_fusion.8
  94.2 0.1 slice_bitcast_fusion
  94.2 0.1 convert_reduce_fusion.1
  94.3 0.7 fusion.28
  95.0 1.2 fusion.19
  96.1 0.2 convert_reduce_fusion
  96.3 0.7 fusion.18
  97.0 0.7 select_reduce_fusion
  97.6 0.0 all-gather.6.cloned.1.call-done.blocks_ref
  97.6 0.0 all-gather.4.cloned.1.call-done
  97.6 1.1 slice.23
  98.7 4.1 %convolution_convert_fusion = bf16[3584,128]{1,0:T(8,128)(2,1)} fusion(bf16[4096,512]{1,0:T(8,128)(2,1)} %all-gather.4.cloned.1.call-done, bf16[512,512]{1,0:T(8,128)(2,1)S(1)} %slice.23, s32[]{:T(128)S(6)} %select_n.68), kind=kOutput, calls=%fused_computation | convolution fusion | flops 470220800 | bytes 4718596 | tf_op jit(solution)/shard_map/dot_general | solution.py:438
  102.8 8.5 %shard_map.96 = bf16[112,128,128]{2,1,0:T(8,128)(2,1)} custom-call(s32[112]{0:T(128)} %get-tuple-element.22.slot_ref, s32[112]{0:T(128)} %get-tuple-element.21.brow_ref, bf16[112,128,128]{2,1,0:T(8,128)(2,1)} %all-gather.6.cloned.1.call-done.blocks_ref, bf16[28,128,128]{2,1,0:T(8,128)(2,1)} %bitcast.48), custom_call_target="tpu_custom_call" | custom-call | flops 469762048 | bytes 8257536 | tf_op jit(solution)/shard_map/pallas_call | solution.py:14
  111.3 4.5 %all-to-all-start = ((bf16[112,128,128]{2,1,0:T(8,128)(2,1)}), bf16[112,128,128]{2,1,0:T(8,128)(2,1)}, u32[]{:S(2)}, u32[]{:S(2)}) async-start(bf16[112,128,128]{2,1,0:T(8,128)(2,1)} %shard_map.96), calls=%async_computation | async-start | bytes 7340032 | tf_op jit(solution)/shard_map/all_to_all | solution.py:448
  115.9 0.0 all-gather.8.cloned.1.call-start
  115.9 1.2 broadcast_select_fusion.brow_ref
  117.1 0.0 copy-start.2
  117.1 9.5 %shard_map.95 = bf16[28,128,128]{2,1,0:T(8,128)(2,1)} custom-call(s32[112]{0:T(128)} %get-tuple-element.28.position_ref, s32[112]{0:T(128)} %broadcast_select_fusion.brow_ref, bf16[112,128,128]{2,1,0:T(8,128)(2,1)} %all-gather.6.cloned.1.call-done.blocks_ref, bf16[224,128,128]{2,1,0:T(8,128)(2,1)} %bitcast.46), custom_call_target="tpu_custom_call" | custom-call | flops 469762048 | bytes 11927552 | tf_op jit(solution)/shard_map/pallas_call | solution.py:14
  126.6 0.0 copy-start.1
  126.6 0.0 all-gather.8.cloned.1.call-update
  126.6 1.1 slice_reduce_fusion
  127.8 1.1 slice_divide_fusion
  128.9 0.1 fusion.9
  129.0 0.2 convolution_convert_fusion.2
  129.2 0.3 select_reduce_fusion.2
  129.5 0.1 copy.31
  129.6 0.6 sub.25.asked_ref
  130.2 29.9 %all-gather.8.cloned.1.call-done = bf16[3584,512]{1,0:T(8,128)(2,1)} async-done(((bf16[3584,128]{1,0:T(8,128)(2,1)}), bf16[3584,512]{1,0:T(8,128)(2,1)}) %all-gather.8.cloned.1.call-update) | async-done | bytes 3670032 | tf_op jit(solution)/shard_map/all_gather | solution.py:458
  160.1 0.0 copy-done.2
  160.1 0.0 copy-start
  160.1 4.2 %convolution_convert_fusion.1 = bf16[3584,128]{1,0:T(8,128)(2,1)} fusion(bf16[3584,512]{1,0:T(8,128)(2,1)} %all-gather.8.cloned.1.call-done, bf16[512,128]{1,0:T(8,128)(2,1)S(1)} %copy-done.2), kind=kOutput, calls=%fused_computation.1 | convolution fusion | flops 470220800 | bytes 4718592 | tf_op jit(solution)/shard_map/dot_general | solution.py:459
  164.3 0.0 copy-done.1
  164.3 0.0 copy-done
  164.3 1.2 fusion.23.refs_0_
  165.5 40.9 %shard_map.97 = f32[512,128]{1,0:T(8,128)S(1)} custom-call(f32[512,128]{1,0:T(8,128)S(1)} %fusion.23.refs_0_), custom_call_target="tpu_custom_call" | custom-call | flops 65536 | bytes 1048576 | tf_op jit(solution)/shard_map/pallas_call | solution.py:169
  206.4 0.0 all-to-all-done.returned_ref
  206.4 0.7 broadcast_multiply_fusion
  207.2 5.6 %shard_map.98 = bf16[28,128,128]{2,1,0:T(8,128)(2,1)} custom-call(s32[112]{0:T(128)} %sub.25.asked_ref, s32[1,128]{1,0:T(1,128)} %held_ref.1, bf16[112,128,128]{2,1,0:T(8,128)(2,1)} %all-to-all-done.returned_ref), custom_call_target="tpu_custom_call" | custom-call | bytes 4588032 | tf_op jit(solution)/shard_map/pallas_call | solution.py:14
  (4 shorter events, 0.0 us)
Async XLA Ops:
  7.2 3.1 %copy-start.4 = (s32[1,29]{1,0:T(1,128)S(1)}, s32[1,29]{1,0:T(1,128)}, u32[]{:S(2)}) copy-start(s32[1,29]{1,0:T(1,128)} %param.9) | copy-start | bytes 352
  7.2 3.7 %copy-start.3 = (s32[1,112]{1,0:T(1,128)S(1)}, s32[1,112]{1,0:T(1,128)}, u32[]{:S(2)}) copy-start(s32[1,112]{1,0:T(1,128)} %param.10) | copy-start | bytes 1348
  7.2 90.5 %all-gather.6.cloned.1.call-start = ((), (), s32[]{:S(2)}) async-start(), calls=%async_computation.2 | async-start | bytes 4587520 | tf_op jit(solution)/shard_map/all_gather | solution.py:395
  7.9 89.7 %all-gather.4.cloned.1.call-start = ((), (), s32[]{:S(2)}) async-start(), calls=%async_computation.1 | async-start | bytes 5242880 | tf_op jit(solution)/shard_map/all_gather | solution.py:394
  111.3 95.1 %all-to-all-start = ((bf16[112,128,128]{2,1,0:T(8,128)(2,1)}), bf16[112,128,128]{2,1,0:T(8,128)(2,1)}, u32[]{:S(2)}, u32[]{:S(2)}) async-start(bf16[112,128,128]{2,1,0:T(8,128)(2,1)} %shard_map.96), calls=%async_computation | async-start | bytes 7340032 | tf_op jit(solution)/shard_map/all_to_all | solution.py:448
  115.9 44.2 %all-gather.8.cloned.1.call-start = ((), (), s32[]{:S(2)}) async-start(), calls=%async_computation.3 | async-start | bytes 4587520 | tf_op jit(solution)/shard_map/all_gather | solution.py:458
  117.1 42.9 %copy-start.2 = (bf16[512,128]{1,0:T(8,128)(2,1)S(1)}, bf16[512,128]{1,0:T(8,128)(2,1)}, u32[]{:S(2)}) copy-start(bf16[512,128]{1,0:T(8,128)(2,1)} %param.12) | copy-start | bytes 393220
  126.6 37.7 %copy-start.1 = (bf16[3584,128]{1,0:T(8,128)(2,1)S(1)}, bf16[3584,128]{1,0:T(8,128)(2,1)}, u32[]{:S(2)}) copy-start(bf16[3584,128]{1,0:T(8,128)(2,1)} %param.13) | copy-start | bytes 2752516
  160.1 4.2 %copy-start = (bf16[3584,512]{1,0:T(8,128)(2,1)S(1)}, bf16[3584,512]{1,0:T(8,128)(2,1)}, u32[]{:S(2)}) copy-start(bf16[3584,512]{1,0:T(8,128)(2,1)} %all-gather.8.cloned.1.call-done) | copy-start | bytes 11010052
Sparse Core Ops, SparseCore 0:
  9.6 34.2 all-gather.5
  45.4 34.9 all-gather.3
  126.7 33.2 all-gather.7
